TPU v7x, 256 devices: a whole 4x4x8 slice. The times are simulated.
256 devices in a mesh: tgt: 8 (over y, x_hi), sup: 32 (over z, x_lo, core).
Axes of the slice: x: 4 (x_hi: 2, x_lo: 2; x = x_hi * 2 + x_lo), y: 4, z: 8, core: 2. Of those that a mesh axis runs over, the one named last changes fastest.
Arguments:
- support: float32 [256, 3, 1024], P(('tgt', 'sup')), may hold values from -6 to 6
- support_labels: int32 [256], replicated, may hold values from 0 to 9
- targets: float32 [256, 3, 1024], P('tgt'), may hold values from -6 to 6
- target_labels: int32 [256], P('tgt'), may hold values from 0 to 9
Outputs:
- support_grad: float32 [256, 3, 1024], P(('tgt', 'sup'))
- objective: float32 [], replicated
All inputs are finite; a program needn't handle non-finite values.
Results may differ from a plain program's by a relative error of at most 0.0003.
Values sent between devices are 32-bit elements; how exact they have to be, the bound alone decides.
No kernel may reach another device: no remote copies, remote signals or barrier semaphores. Data moves between devices by JAX's collectives and lax.ppermute only.
A program may use at most 128 MiB of HBM per device.

v0:
```python
import jax
import jax.numpy as jnp
from jax import lax
from jax.sharding import PartitionSpec as P

SIDE = 32
CLASSES = 10


def stencil(maps):
    column = jnp.arange(maps.shape[-1], dtype=jnp.int32) % SIDE
    zero_col = jnp.zeros(maps.shape[:-1] + (1,), maps.dtype)
    from_left = jnp.concatenate([zero_col, maps[..., :-1]], axis=-1) * (column != 0).astype(
        maps.dtype
    )
    from_right = jnp.concatenate([maps[..., 1:], zero_col], axis=-1) * (column != SIDE - 1).astype(
        maps.dtype
    )
    across = maps + from_left + from_right
    zero_row = jnp.zeros(maps.shape[:-1] + (SIDE,), maps.dtype)
    from_above = jnp.concatenate([zero_row, across[..., :-SIDE]], axis=-1)
    from_below = jnp.concatenate([across[..., SIDE:], zero_row], axis=-1)
    return across + from_above + from_below


def arc_maps(sigmas, var_left, var_right):
    scales = jnp.sqrt(var_left * var_right)
    cosine = jnp.clip(sigmas / scales, -0.9999, 0.9999)
    remain = jnp.pi - jnp.arccos(cosine)
    expect = scales * (jnp.sqrt(1.0 - cosine * cosine) + remain * cosine) / (2.0 * jnp.pi)
    slopes = remain / (2.0 * jnp.pi)
    return (expect, slopes)


def self_vars(images):
    first = 2.0 / 27.0 * stencil(jnp.sum(images * images, axis=1)) + 0.1
    result = [first]
    result.append(2.0 / 9.0 * stencil(0.5 * result[-1]) + 0.1)
    return result


def ntk_block(left, right):
    vars_left = self_vars(left)
    vars_right = self_vars(right)
    crossed = jnp.sum(left[:, None] * right[None], axis=2)
    sigmas = 2.0 / 27.0 * stencil(crossed) + 0.1
    thetas = sigmas
    expect, slopes = arc_maps(sigmas, vars_left[0][:, None], vars_right[0][None])
    sigmas = 2.0 / 9.0 * stencil(expect) + 0.1
    thetas = sigmas + 2.0 / 9.0 * stencil(slopes * thetas)
    expect, slopes = arc_maps(sigmas, vars_left[-1][:, None], vars_right[-1][None])
    return 2.0 / left.shape[-1] * jnp.sum(expect + slopes * thetas, axis=-1)


def one_hot(labels):
    return (labels[:, None] == jnp.arange(CLASSES, dtype=jnp.int32)[None]).astype(jnp.float32) - 0.1


def turned(matrix, shift, axis_dim):
    doubled = jnp.concatenate([matrix, matrix], axis=axis_dim)
    return lax.dynamic_slice_in_dim(doubled, shift, matrix.shape[axis_dim], axis_dim)


def on_device(support, support_labels, targets, target_labels):
    block_count = lax.axis_size(("tgt", "sup"))
    self_index = lax.axis_index(("tgt", "sup"))
    own_count = support.shape[0]
    gathered = lax.all_gather(support, ("tgt", "sup"), axis=0, tiled=True)
    total = gathered.shape[0]
    group_rows = 32 * own_count
    own_begin = self_index * own_count
    back_shift = (total - own_begin) % total
    rotated = turned(gathered, own_begin, 0)

    def keep_mask(offsets):
        return offsets < block_count - self_index

    group_count = ((block_count - self_index) * own_count + group_rows - 1) // group_rows

    def forward_group(step_index, rows_rot):
        begin_row = step_index * group_rows
        others = lax.dynamic_slice_in_dim(rotated, begin_row, group_rows, 0)
        offsets = (begin_row + jnp.arange(group_rows, dtype=jnp.int32)) // own_count
        weights = jnp.where(keep_mask(offsets), jnp.where(offsets == 0, 0.5, 1.0), 0.0).astype(
            jnp.float32
        )
        values = ntk_block(support, others) * weights[None, :]
        return lax.dynamic_update_slice_in_dim(rows_rot, values, begin_row, 1)

    rows_rot = lax.fori_loop(
        0, group_count, forward_group, jnp.zeros((own_count, total), jnp.float32)
    )
    rows_abs = turned(rows_rot, back_shift, 1)
    placed = lax.dynamic_update_slice_in_dim(
        jnp.zeros((total, total), jnp.float32), rows_abs, own_begin, 0
    )
    kernel_ss = lax.psum(placed + placed.T, ("tgt", "sup"))
    support_hot = one_hot(support_labels)

    def fit_coeffs(kernel):
        ridge = 0.1 * jnp.trace(kernel) / kernel.shape[0]
        factor = jnp.linalg.cholesky(kernel + ridge * jnp.eye(kernel.shape[0], dtype=jnp.float32))
        return jax.scipy.linalg.cho_solve((factor, True), support_hot)

    coeffs, coeff_back = jax.vjp(fit_coeffs, kernel_ss)
    grad_local = jnp.zeros_like(support)
    target_all, labels_all = (
        lax.all_gather(targets, "tgt", axis=0, tiled=True),
        lax.all_gather(target_labels, "tgt", axis=0, tiled=True),
    )
    count = target_all.shape[0]
    stacked = target_all.reshape((count // 64, 64) + target_all.shape[1:])
    kernel_ts = lax.map(lambda piece: ntk_block(piece, support), stacked).reshape(count, own_count)
    coeff_own = lax.dynamic_slice_in_dim(coeffs, own_begin, own_count, 0)
    predicted = lax.psum(
        jnp.dot(kernel_ts, coeff_own, precision=lax.Precision.HIGHEST), ("tgt", "sup")
    )
    residual = predicted - one_hot(labels_all)
    objective = 0.5 * jnp.sum(residual * residual)
    fitted_own = jnp.dot(kernel_ts.T, residual, precision=lax.Precision.HIGHEST)
    fitted_all = lax.all_gather(fitted_own, ("tgt", "sup"), axis=0, tiled=True)
    grad_ts = jnp.dot(residual, coeff_own.T, precision=lax.Precision.HIGHEST)

    def target_step(step_index, accum):
        begin_row = step_index * 64
        piece = lax.dynamic_slice_in_dim(target_all, begin_row, 64, 0)
        cotangent = lax.dynamic_slice_in_dim(grad_ts, begin_row, 64, 0)
        _, back_fn = jax.vjp(lambda images: ntk_block(piece, images), support)
        return accum + back_fn(cotangent)[0]

    grad_local = lax.fori_loop(0, count // 64, target_step, grad_local)
    grad_ss = coeff_back(fitted_all)[0]
    grad_rows = lax.dynamic_slice_in_dim(grad_ss, own_begin, own_count, 0)
    grad_cols_t = lax.dynamic_slice_in_dim(grad_ss, own_begin, own_count, 1).T
    paired_abs = grad_rows + grad_cols_t
    plain_rot = turned(grad_rows, own_begin, 1)
    paired_rot = turned(paired_abs, own_begin, 1)

    def backward_group(step_index, carry):
        own_accum, rot_accum = carry
        begin_row = step_index * group_rows
        others = lax.dynamic_slice_in_dim(rotated, begin_row, group_rows, 0)
        offsets = (begin_row + jnp.arange(group_rows, dtype=jnp.int32)) // own_count
        plain_part = lax.dynamic_slice_in_dim(plain_rot, begin_row, group_rows, 1)
        paired_part = lax.dynamic_slice_in_dim(paired_rot, begin_row, group_rows, 1)
        cotangent = jnp.where(offsets[None, :] == 0, plain_part, paired_part)
        cotangent = cotangent * keep_mask(offsets).astype(jnp.float32)[None, :]
        _, back_fn = jax.vjp(ntk_block, support, others)
        d_own, d_others = back_fn(cotangent)
        current = lax.dynamic_slice_in_dim(rot_accum, begin_row, group_rows, 0)
        rot_accum = lax.dynamic_update_slice_in_dim(rot_accum, current + d_others, begin_row, 0)
        return (own_accum + d_own, rot_accum)

    own_part, grad_rot = lax.fori_loop(
        0, group_count, backward_group, (grad_local, jnp.zeros_like(gathered))
    )
    grad_abs = turned(grad_rot, back_shift, 0)
    result = own_part + lax.psum_scatter(grad_abs, ("tgt", "sup"), scatter_dimension=0, tiled=True)
    return (result, objective)


def solution(mesh):
    placed = (P(("tgt", "sup"), None, None), P(), P("tgt", None, None), P("tgt"))
    return jax.shard_map(
        on_device,
        mesh=mesh,
        in_specs=placed,
        out_specs=(P(("tgt", "sup"), None, None), P()),
        check_vma=False,
    )
```

profile of v0, /device:TPU:1, one launch (start us, length us, event | category | flops | bytes accessed | tf_op | source)
XLA Modules:
  0.0 1429.8 jit_solution(9859887872602133092)
XLA Ops:
  13.1 11.4 all-reduce.145
  25.3 401.5 %all-gather.6.cloned.1.call-done = f32[256,3,1024]{2,1,0:T(4,128)} async-done(((f32[1,3,1024]{2,1,0:T(4,128)}), f32[256,3,1024]{2,1,0:T(4,128)}) %all-gather.6.cloned.1.call-update) | async-done | bytes 3145744 | tf_op jit(solution)/shard_map/all_gather | solution.py:68
  426.8 8.8 fusion.121
  435.6 41.4 %while.66 = (s32[]{:T(128)}, f32[1,256]{1,0:T(1,128)S(1)}, s32[]{:T(128)}, f32[1024]{0:T(1024)S(1)}, f32[1,1024]{1,0:T(1,128)S(1)}, /*index=5*/f32[1,1024]{1,0:T...) while((s32[]{:T(128)}, f32[1,256]{1,0:T(1,128)S(1)}, ...), condition=%wide.region_10.11_spmd, body=%wide.region_6.10_spmd.sunk | while | flops 2799814 | bytes 11193903 | solution.py:90
  479.0 16.2 %all-gather.4.cloned.1.call-done = f32[256,3,1024]{2,0,1:T(8,128)} async-done(((f32[32,3,1024]{2,0,1:T(8,128)}), f32[256,3,1024]{2,0,1:T(8,128)}) %all-gather.4.cloned.1.call-update) | async-done | bytes 3145744 | tf_op jit(solution)/shard_map/all_gather | solution.py:108
  495.2 33.2 %while.65 = (s32[]{:T(128)}, f32[4,64,1]{1,2,0:T(1,128)S(1)}, f32[4,64,3,1024]{3,1,0,2:T(8,128)}, f32[1024]{0:T(1024)S(1)}, f32[1,1024]{1,0:T(1,128)S(1)}, /*ind...) while((s32[]{:T(128)}, f32[4,64,1]{1,2,0:T(1,128)S(1)}, ...), condition=%wide.region_5.6_spmd, body=%wide.region_1.5_spmd.sunk | while | flops 5552130 | bytes 24568152 | solution.py:113
  529.6 218.3 %all-reduce.151.cloned.1.call-done = f32[256,256]{1,0:T(8,128)} async-done(((f32[256,256]{1,0:T(8,128)}), f32[256,256]{1,0:T(8,128)}) %all-reduce.151.cloned.1.call-update) | async-done | bytes 262160 | tf_op jit(solution)/shard_map/psum | solution.py:97
  752.2 11.7 cholesky.49
  764.6 9.8 custom-call.24
  774.9 11.7 cholesky.103
  788.7 3.9 while.70
  792.7 19.9 %custom-call.30 = f32[2,128,128]{1,2,0:T(8,128)S(1)} custom-call(f32[2,128,128]{2,1,0:T(8,128)S(1)} %get-tuple-element.633), custom_call_target="InvertDiagBlocksLowerTriangular" | custom-call | tf_op jit(solution)/shard_map/jvp(jit(_cho_solve))/triangular_solve/custom-call.0 | solution.py:103
  814.0 77.5 %psum.15 = f32[256,10]{0,1:T(8,128)S(1)} all-reduce(f32[256,10]{0,1:T(8,128)S(1)} %broadcast_multiply_fusion.12), channel_id=1, replica_groups=mesh['tgt'=8,'sup'=32] {'tgt','sup'}, use_global_device_ids=true, to_apply=%region_17.20 | all-reduce | flops 2560 | bytes 20480 | tf_op jit(solution)/shard_map/psum | solution.py:115
  892.0 73.4 %all-reduce.146 = f32[2560]{0:T(1024)S(1)} all-reduce(f32[2560]{0:T(1024)S(1)} %dynamic-update-slice.19), channel_id=2, replica_groups=mesh['tgt'=8,'sup'=32] {'tgt','sup'}, use_global_device_ids=true, to_apply=%add.146 | all-reduce | flops 2560 | bytes 20480
  967.0 3.9 while.68
  970.9 19.7 %custom-call.25 = f32[2,128,128]{1,2,0:T(8,128)S(1)} custom-call(f32[2,128,128]{2,1,0:T(8,128)S(1)} %get-tuple-element.586), custom_call_target="InvertDiagBlocksLowerTriangular" | custom-call | tf_op jit(solution)/shard_map/transpose(jvp(jit(cholesky)))/triangular_solve | solution.py:102
  990.6 54.2 %while.69 = (s32[]{:T(128)}, f32[1,3,1024]{2,1,0:T(4,128)S(1)}, f32[256,3,1024]{2,0,1:T(8,128)}, f32[1,3,1024]{2,1,0:T(4,128)S(1)}, f32[1024]{0:T(1024)S(1)}, /*...) while((s32[]{:T(128)}, f32[1,3,1024]{2,1,0:T(4,128)S(1)}, ...), condition=%wide.region_24.28_spmd.clone, body=%wide.region_18.27_spmd.clone.sunk | while | flops 14434051 | bytes 40932200 | solution.py:131
  1050.1 3.1 broadcast_in_dim.254
  1053.2 95.8 %while.67 = (s32[]{:T(128)}, f32[1,3,1024]{2,1,0:T(4,128)S(1)}, f32[256,3,1024]{2,1,0:T(4,128)}, s32[]{:T(128)}, f32[1,3,1024]{2,1,0:T(4,128)S(1)}, /*index=5*/f...) while((s32[]{:T(128)}, f32[1,3,1024]{2,1,0:T(4,128)S(1)}, ...), condition=%wide.region_32.37_spmd, body=%wide.region_26.36_spmd.sunk | while | flops 9614242 | bytes 27091312 | solution.py:154
  1074.7 2.3 fusion.443
  1134.5 2.4 fusion.443
  1146.5 2.4 fusion.443
  1149.0 8.8 fusion.120
  1159.2 261.4 %all-reduce.153.cloned.1.call-done = f32[256,3,1024]{2,1,0:T(4,128)} async-done(((f32[256,3,1024]{2,1,0:T(4,128)}), f32[256,3,1024]{2,1,0:T(4,128)}) %all-reduce.153.cloned.1.call-update) | async-done | bytes 3145744
  (1143 shorter events, 243.5 us)
Async XLA Ops:
  7.2 419.6 %all-gather.6.cloned.1.call-start = ((), (), s32[]{:S(2)}) async-start(), calls=%async_computation.1 | async-start | bytes 4210688 | tf_op jit(solution)/shard_map/all_gather | solution.py:68
  8.5 486.6 %all-gather.4.cloned.1.call-start = ((), (), s32[]{:S(2)}) async-start(), calls=%async_computation | async-start | bytes 3538944 | tf_op jit(solution)/shard_map/all_gather | solution.py:108
  9.3 738.6 %all-reduce.151.cloned.1.call-start = ((), (), s32[]{:S(2)}) async-start(), calls=%async_computation.2 | async-start | bytes 524288 | tf_op jit(solution)/shard_map/psum | solution.py:97
  25.3 410.3 %copy-start = (f32[1,3,1024]{2,1,0:T(4,128)S(1)}, f32[1,3,1024]{2,1,0:T(4,128)}, u32[]{:S(2)}) copy-start(f32[1,3,1024]{2,1,0:T(4,128)} %copy.56) | copy-start | bytes 36868
  478.0 0.7 copy-start.1
  478.7 941.8 %all-reduce.153.cloned.1.call-start = ((), (), s32[]{:S(2)}) async-start(), calls=%async_computation.3 | async-start | bytes 8388608
Sparse Core Ops, SparseCore 0:
  9.9 416.8 all-gather.5
  429.4 65.7 all-gather.3
  500.6 247.1 all-reduce.150
  1158.0 262.4 all-reduce.152
where the time goes:
time: 1440 us; the launch traced here: 1430 us
  waiting for transfers between devices  898 us (62%)
  other arithmetic  268 us (19%)
  blocking collectives  162 us (11%)
  local copies, waits for them, and re-layouts  68.4 us (5%)
  between operations  19.3 us (1%)
    all_gather x1, waiting for transfers between devices, on_device(): gathered = lax.all_gather(support, ('tgt', 'sup'), axis=0, tiled=True)  401 us
    unnamed x5, waiting for transfers between devices  262 us
    psum x1, waiting for transfers between devices, on_device(): kernel_ss = lax.psum(placed + placed.T, ('tgt', 'sup'))  218 us
    unnamed x2, blocking collectives  84.8 us
    psum x1, blocking collectives, on_device(): lax.psum(jnp.dot(kernel_ts, coeff_own, precision=lax.Precision.HIGHEST),...  77.5 us
    another operation x9, other arithmetic, fit_coeffs(): jnp.linalg.cholesky(kernel + ridge * jnp.eye(kernel.shape[0], dtype=jnp.f...  54.4 us
    reduce_sum x28, other arithmetic, ntk_block(): crossed = jnp.sum(left[:, None] * right[None], axis=2)  40.7 us
  transfers between devices with their start and end apart: 4, of which 4 were waited for; matrix products, arithmetic and copies ran while one was open for 6% of the time, Pallas kernels for 0%

commit v1 on v0

v1 whole, which is shorter than its diff:
```python
import functools
import math

import jax
import jax.numpy as jnp
from jax import lax
from jax.experimental import pallas as pl
from jax.experimental.pallas import tpu as pltpu
from jax.sharding import PartitionSpec as P

SIDE = 32
CLASSES = 10
BOTH = ("tgt", "sup")
LANES = 128
FOUR = 4
ALPHA1 = (2.0 / 9.0) / (2.0 * math.pi)
ALPHA2 = 1.0 / (2.0 * math.pi)
FIRST = 2.0 / 27.0
SECOND = 2.0 / 9.0
ACOS = (
    1.5707963050,
    -0.2145988016,
    0.0889789874,
    -0.0501743046,
    0.0308918810,
    -0.0170881256,
    0.0066700901,
    -0.0012624911,
)
VMEM_LIMIT = 56 * 1024 * 1024
HIGHEST = lax.Precision.HIGHEST


def lane_index(shape):
    return lax.broadcasted_iota(jnp.int32, shape, len(shape) - 1)


def across(x, keep_left, keep_right):
    axis = x.ndim - 1
    return x + pltpu.roll(x, 1, axis) * keep_left + pltpu.roll(x, LANES - 1, axis) * keep_right


def edge_masks(shape):
    column = lane_index(shape) % SIDE
    return (column != 0).astype(jnp.float32), (column != SIDE - 1).astype(jnp.float32)


def swap_blocks(x0, x1, x2, x3):
    lane = lane_index(x0.shape)
    low = lane < 64
    even = (lane // SIDE) % 2 == 0
    axis = x0.ndim - 1
    a0 = jnp.where(low, x0, pltpu.roll(x2, 64, axis))
    a2 = jnp.where(low, pltpu.roll(x0, 64, axis), x2)
    a1 = jnp.where(low, x1, pltpu.roll(x3, 64, axis))
    a3 = jnp.where(low, pltpu.roll(x1, 64, axis), x3)
    y0 = jnp.where(even, a0, pltpu.roll(a1, 32, axis))
    y1 = jnp.where(even, pltpu.roll(a0, 96, axis), a1)
    y2 = jnp.where(even, a2, pltpu.roll(a3, 32, axis))
    y3 = jnp.where(even, pltpu.roll(a2, 96, axis), a3)
    return y0, y1, y2, y3


def spread_blocks(y):
    lane = lane_index(y.shape)
    low = lane < 64
    even = (lane // SIDE) % 2 == 0
    axis = y.ndim - 1
    turned = pltpu.roll(y, 64, axis)
    first = jnp.where(low, y, turned)
    last = jnp.where(low, turned, y)
    first_turned = pltpu.roll(first, 32, axis)
    last_turned = pltpu.roll(last, 32, axis)
    return (
        jnp.where(even, first, first_turned),
        jnp.where(even, first_turned, first),
        jnp.where(even, last, last_turned),
        jnp.where(even, last_turned, last),
    )


def column_kernel(images_ref, pack_ref):
    keep_left, keep_right = edge_masks((8, LANES))
    for c in range(3):
        for s in range(8):
            y = images_ref[pl.ds(c * 8 + s, 8, stride=32), :]
            for k, z in enumerate(spread_blocks(y)):
                pack_ref[c, 4 * s + k] = z
    sums = []
    for r in range(SIDE):
        b0, b1, b2 = pack_ref[0, r], pack_ref[1, r], pack_ref[2, r]
        sums.append(across(b0 * b0 + b1 * b1 + b2 * b2, keep_left, keep_right))
    variances = []
    for r in range(SIDE):
        total = sums[r]
        if r > 0:
            total = total + sums[r - 1]
        if r < SIDE - 1:
            total = total + sums[r + 1]
        q = FIRST * total + 0.1
        inverse = lax.rsqrt(q)
        pack_ref[3, r] = inverse
        pack_ref[4, r] = q * inverse
        variances.append(across(q, keep_left, keep_right))
    for r in range(SIDE):
        total = variances[r]
        if r > 0:
            total = total + variances[r - 1]
        if r < SIDE - 1:
            total = total + variances[r + 1]
        q = (0.5 * SECOND) * total + 0.1
        inverse = lax.rsqrt(q)
        pack_ref[5, r] = inverse
        pack_ref[6, r] = q * inverse


def arc(sigma, inverse, scale, alpha, bump):
    raw = sigma * inverse
    if bump is not None:
        raw = raw + bump
    cosine = jnp.minimum(jnp.maximum(raw, -0.9999), 0.9999)
    inside = cosine == raw
    size = jnp.abs(cosine)
    below = 1.0 - size
    poly = jnp.float32(alpha * ACOS[-1])
    for coefficient in ACOS[-2::-1]:
        poly = poly * size + jnp.float32(alpha * coefficient)
    angle = (below * lax.rsqrt(below)) * poly
    slope = jnp.where(cosine >= 0.0, jnp.float32(alpha * math.pi) - angle, angle)
    rest = 1.0 - cosine * cosine
    root = alpha * lax.rsqrt(rest)
    value = scale * (rest * root + slope * cosine)
    return value, slope, root * inverse, inside


def maps_kernel(
    place_ref, images_ref, pack_ref, entries_ref, units_ref, planes_ref, rows_ref, *, diagonal
):
    group = pl.program_id(0)
    keep_left, keep_right = edge_masks((8, LANES))
    sublane = lax.broadcasted_iota(jnp.int32, (8, LANES), 0)

    for c in range(3):
        planes = swap_blocks(*[images_ref[i, c] for i in range(FOUR)])
        for k in range(FOUR):
            rows_ref[c, k] = planes[k]

    def down(planes):
        result = []
        for k in range(FOUR):
            above = planes[k - 1]
            if k == 0:
                above = jnp.where(sublane == 0, 0.0, pltpu.roll(planes[FOUR - 1], 1, 0))
            under = planes[(k + 1) % FOUR]
            if k == FOUR - 1:
                under = jnp.where(sublane == 7, 0.0, pltpu.roll(planes[0], 7, 0))
            result.append(planes[k] + above + under)
        return result

    squares = [
        across(sum(rows_ref[c, k] * rows_ref[c, k] for c in range(3)), keep_left, keep_right)
        for k in range(FOUR)
    ]
    first = [FIRST * t + 0.1 for t in down(squares)]
    second = [
        (0.5 * SECOND) * t + 0.1 for t in down([across(q, keep_left, keep_right) for q in first])
    ]
    for k in range(FOUR):
        inverse1 = lax.rsqrt(first[k])
        inverse2 = lax.rsqrt(second[k])
        rows_ref[3, k] = inverse1
        rows_ref[4, k] = first[k] * inverse1
        rows_ref[5, k] = inverse2
        rows_ref[6, k] = second[k] * inverse2
    for c in range(3):
        for k in range(FOUR):
            plane = FIRST * rows_ref[c, k]
            rows_ref[c, k] = plane
            planes_ref[0, c, k] = plane

    def row(c, r):
        return jnp.broadcast_to(rows_ref[c, r % FOUR, pl.ds(r // FOUR, 1), :], (8, LANES))

    bump = None
    if diagonal:
        own_row = place_ref[1]
        image = group * FOUR + lane_index((8, LANES)) // SIDE
        own = jnp.logical_and(image == own_row, sublane == place_ref[0])
        bump = own.astype(jnp.float32)

    def vertical(window, r):
        total = window[r]
        if r > 0:
            total = total + window[r - 1]
        if r < SIDE - 1:
            total = total + window[r + 1]
        return total

    cross, value_sum, slope_sum, dsig_sum, ds2_sum, dtheta_sum = {}, {}, {}, {}, {}, {}
    kept = {}
    total = jnp.zeros((8, LANES), jnp.float32)
    for step in range(SIDE + 4):
        r = step
        if r < SIDE:
            x = row(0, r) * pack_ref[0, r] + row(1, r) * pack_ref[1, r] + row(2, r) * pack_ref[2, r]
            cross[r] = across(x, keep_left, keep_right)
        r = step - 1
        if 0 <= r < SIDE:
            sigma = vertical(cross, r) + 0.1
            inverse = row(3, r) * pack_ref[3, r]
            scale = row(4, r) * pack_ref[4, r]
            value, slope, weight, inside = arc(sigma, inverse, scale, ALPHA1, None)
            value_sum[r] = across(value, keep_left, keep_right)
            slope_sum[r] = across(slope * sigma, keep_left, keep_right)
            kept[r] = (
                sigma,
                value,
                slope,
                jnp.where(inside, slope, 0.0),
                jnp.where(inside, sigma * weight, 0.0),
            )
        r = step - 2
        if 0 <= r < SIDE:
            sigma = vertical(value_sum, r) + 0.1
            theta = sigma + vertical(slope_sum, r)
            inverse = row(5, r) * pack_ref[5, r]
            scale = row(6, r) * pack_ref[6, r]
            value, slope, weight, inside = arc(sigma, inverse, scale, ALPHA2, bump)
            total = total + (value + slope * theta)
            dsigma = jnp.where(inside, slope + theta * weight, 0.0)
            units_ref[0, 2, r] = value - dsigma * sigma
            ds2_sum[r] = across(slope, keep_left, keep_right)
            dsig_sum[r] = across(dsigma + slope, keep_left, keep_right)
        r = step - 3
        if 0 <= r < SIDE:
            sigma, value, slope, slope_in, weight_in = kept.pop(r)
            dvalue = vertical(dsig_sum, r)
            dproduct = vertical(ds2_sum, r)
            inner = slope_in * dvalue + dproduct * weight_in
            units_ref[0, 1, r] = value * dvalue - inner * sigma
            dtheta_sum[r] = across(inner + dproduct * slope, keep_left, keep_right)
        r = step - 4
        if 0 <= r < SIDE:
            units_ref[0, 0, r] = vertical(dtheta_sum, r)

    lane = lane_index((LANES, LANES))
    pick = lane == group * FOUR + lax.broadcasted_iota(jnp.int32, (LANES, LANES), 0) // SIDE
    part = jnp.dot(
        total * (2.0 / 1024.0),
        pick.astype(jnp.float32),
        precision=HIGHEST,
        preferred_element_type=jnp.float32,
    )

    @pl.when(group == 0)
    def _():
        entries_ref[...] = part

    @pl.when(group > 0)
    def _():
        entries_ref[...] += part


def halves(x):
    high = x.astype(jnp.bfloat16)
    return high, (x - high.astype(jnp.float32)).astype(jnp.bfloat16)


def product3(a, b):
    (ah, al), (bh, bl) = a, b
    dot = functools.partial(jnp.dot, preferred_element_type=jnp.float32)
    return dot(ah, bh) + (dot(ah, bl) + dot(al, bh))


def exact(a, b):
    return jnp.dot(a, b, precision=HIGHEST, preferred_element_type=jnp.float32)


def exact_nt(a, b):
    return lax.dot_general(
        a,
        b,
        (((1,), (1,)), ((), ())),
        precision=HIGHEST,
        preferred_element_type=jnp.float32,
    )


def solve_kernel(
    place_ref,
    received_ref,
    support_labels_ref,
    target_labels_ref,
    pack_ref,
    units_t_hbm,
    units_s_hbm,
    planes_t_ref,
    planes_s_ref,
    grad_ref,
    objective_ref,
    units_ref,
    kernel_ref,
    cross_ref,
    inverse_ref,
    weights_ref,
    grads_ref,
    sem,
):
    copies = [
        pltpu.make_async_copy(units_t_hbm, units_ref.at[pl.ds(0, 8)], sem.at[0]),
        pltpu.make_async_copy(units_s_hbm, units_ref.at[pl.ds(8, 8)], sem.at[1]),
    ]
    for copy in copies:
        copy.start()

    for which, out_ref in ((0, kernel_ref), (1, cross_ref)):
        for q in range(2):
            for h in range(2):
                blocks = []
                for i in range(FOUR):
                    start = (4 * h + i) * 32 * 4 + 2 * which + q
                    blocks.append(received_ref[pl.ds(start, 32, stride=4), :])
                for j, y in enumerate(swap_blocks(*blocks)):
                    out_ref[pl.ds((4 * q + j) * 32, 32), pl.ds(h * LANES, LANES)] = y

    count = 256
    matrix = kernel_ref[...]
    row_id = lax.broadcasted_iota(jnp.int32, (count, count), 0)
    col_id = lax.broadcasted_iota(jnp.int32, (count, count), 1)
    eye = row_id == col_id
    trace = jnp.sum(jnp.where(eye, matrix, 0.0))
    ridge = 0.1 * trace / count
    matrix = matrix + jnp.where(eye, ridge, 0.0)
    kernel_ref[...] = matrix
    bound = jnp.max(jnp.sum(jnp.abs(matrix), axis=0, keepdims=True))
    spread = (bound - ridge) / (bound + ridge)
    start = 2.0 / (bound + ridge)
    square = spread * spread
    gain = 2.0 / (2.0 - square)
    inverse_ref[...] = (gain * start) * (jnp.where(eye, 2.0, 0.0) - start * matrix)
    matrix_halves = halves(matrix)

    def refine(delta):
        square = delta * delta
        gain = 2.0 / (2.0 - square)
        x = inverse_ref[...]
        x_halves = halves(x)
        error = jnp.where(eye, 1.0, 0.0) - product3(matrix_halves, x_halves)
        inverse_ref[...] = gain * (x + product3(x_halves, halves(error)))
        return square / (2.0 - square)

    lax.while_loop(lambda delta: delta > 3e-3, refine, square / (2.0 - square))
    x = inverse_ref[...]
    inverse = x + exact(x, jnp.where(eye, 1.0, 0.0) - exact(matrix, x))

    def solve(right):
        guess = exact(right, inverse)
        for _ in range(2):
            guess = guess + exact(right - exact(guess, matrix), inverse)
        return guess

    class_id = lax.broadcasted_iota(jnp.int32, (16, count), 0)

    def one_hot(labels):
        hot = (class_id == labels).astype(jnp.float32) - 0.1
        return jnp.where(class_id < CLASSES, hot, 0.0)

    coeffs = solve(one_hot(support_labels_ref[...]))
    cross = cross_ref[...]
    residual = exact(coeffs, cross) - one_hot(target_labels_ref[...])
    objective_ref[...] = jnp.full((8, LANES), 0.5 * jnp.sum(residual * residual), jnp.float32)
    adjoint = solve(exact_nt(residual, cross))
    trace_grad = -jnp.sum(adjoint * coeffs)

    mine_t, mine_s = place_ref[0], place_ref[1]
    ids = lax.broadcasted_iota(jnp.int32, (8, count), 1)
    mine = lax.broadcasted_iota(jnp.int32, (8, count), 0) * 32 + mine_s
    pick_columns = (ids == mine).astype(jnp.float32)
    coeffs_col = exact_nt(pick_columns, coeffs)
    adjoint_col = exact_nt(pick_columns, adjoint)
    pick_rows = (
        lax.broadcasted_iota(jnp.int32, (count, LANES), 0)
        == lax.broadcasted_iota(jnp.int32, (count, LANES), 1) + mine_t * 32
    ).astype(jnp.float32)
    coeffs_row = exact(coeffs, pick_rows)
    adjoint_row = exact(adjoint, pick_rows)
    residual_row = exact(residual, pick_rows)
    pair_ts = exact(coeffs_col, residual_row)
    pair_ss = -(exact(coeffs_col, adjoint_row) + exact(adjoint_col, coeffs_row))
    sub8 = lax.broadcasted_iota(jnp.int32, (8, LANES), 0)
    lane8 = lane_index((8, LANES))
    own = jnp.logical_and(sub8 == mine_t, lane8 == mine_s)
    pair_ss = pair_ss + jnp.where(own, (0.2 / count) * trace_grad, 0.0)
    widen = (
        lax.broadcasted_iota(jnp.int32, (LANES, 1024), 0)
        == lax.broadcasted_iota(jnp.int32, (LANES, 1024), 1) // SIDE
    ).astype(jnp.float32)
    for which, pair in ((0, pair_ts), (1, pair_ss)):
        wide = exact(pair * (2.0 / 1024.0), widen)
        for g in range(8):
            weights_ref[8 * which + g] = wide[:, g * LANES : (g + 1) * LANES]

    for copy in copies:
        copy.wait()

    weights = [weights_ref[g] for g in range(16)]

    def gather_row(s, carry):
        for k in range(FOUR):
            r = s * FOUR + k
            sums = [None] * 5
            for g in range(16):
                planes_ref = planes_t_ref if g < 8 else planes_s_ref
                weight = weights[g]
                dx = weight * units_ref[g, 0, r]
                terms = [
                    dx * jnp.broadcast_to(planes_ref[g % 8, c, k, pl.ds(s, 1), :], (8, LANES))
                    for c in range(3)
                ]
                terms.append(weight * units_ref[g, 1, r])
                terms.append(weight * units_ref[g, 2, r])
                sums = [t if a is None else a + t for a, t in zip(sums, terms)]
            for n, total in enumerate(sums):
                total = total + pltpu.roll(total, 64, 1)
                grads_ref[n, r] = total + pltpu.roll(total, 32, 1)
        return carry

    lax.fori_loop(0, 8, gather_row, 0)

    keep_left, keep_right = edge_masks((8, LANES))

    def vertical(window, r):
        total = window[r]
        if r > 0:
            total = total + window[r - 1]
        if r < SIDE - 1:
            total = total + window[r + 1]
        return total

    second, first = {}, {}
    for r in range(SIDE):
        inverse2 = pack_ref[5, r]
        second[r] = across(0.5 * inverse2 * inverse2 * grads_ref[4, r], keep_left, keep_right)
    for r in range(SIDE):
        inverse1 = pack_ref[3, r]
        dq1 = 0.5 * inverse1 * inverse1 * grads_ref[3, r] + (0.5 * SECOND) * vertical(second, r)
        first[r] = across(dq1, keep_left, keep_right)
    lane = lane8 // SIDE
    for s in range(8):
        scales = [(2.0 * FIRST) * vertical(first, 4 * s + k) for k in range(FOUR)]
        for c in range(3):
            full = [
                grads_ref[c, 4 * s + k] + pack_ref[c, 4 * s + k] * scales[k] for k in range(FOUR)
            ]
            merged = jnp.where(
                lane < 2,
                jnp.where(lane == 0, full[0], full[1]),
                jnp.where(lane == 2, full[2], full[3]),
            )
            grad_ref[pl.ds(c * 8 + s, 8, stride=24), :] = merged


def params():
    return pltpu.CompilerParams(vmem_limit_bytes=VMEM_LIMIT)


def f32(*shape):
    return jax.ShapeDtypeStruct(shape, jnp.float32)


def column_pack(images):
    return pl.pallas_call(
        column_kernel,
        out_shape=f32(7, SIDE, 8, LANES),
        compiler_params=params(),
    )(images)


def pair_maps(place, images, pack, diagonal):
    groups = images.shape[0] // FOUR
    return pl.pallas_call(
        functools.partial(maps_kernel, diagonal=diagonal),
        grid=(groups,),
        in_specs=[
            pl.BlockSpec(memory_space=pltpu.SMEM),
            pl.BlockSpec((FOUR, 3, 8, LANES), lambda g: (g, 0, 0, 0)),
            pl.BlockSpec((7, SIDE, 8, LANES), lambda g: (0, 0, 0, 0)),
        ],
        out_specs=[
            pl.BlockSpec((8, LANES), lambda g: (0, 0)),
            pl.BlockSpec((1, 3, SIDE, 8, LANES), lambda g: (g, 0, 0, 0, 0)),
            pl.BlockSpec((1, 3, FOUR, 8, LANES), lambda g: (g, 0, 0, 0, 0)),
        ],
        out_shape=[
            f32(8, LANES),
            f32(groups, 3, SIDE, 8, LANES),
            f32(groups, 3, FOUR, 8, LANES),
        ],
        scratch_shapes=[pltpu.VMEM((7, FOUR, 8, LANES), jnp.float32)],
        compiler_params=params(),
        cost_estimate=pl.CostEstimate(
            flops=groups * 32 * 1024 * 140, bytes_accessed=4 << 20, transcendentals=0
        ),
    )(place, images, pack)


def solve_and_grad(place, received, support_labels, target_labels, pack, units, planes):
    vmem = pl.BlockSpec(memory_space=pltpu.VMEM)
    return pl.pallas_call(
        solve_kernel,
        in_specs=[pl.BlockSpec(memory_space=pltpu.SMEM)]
        + [vmem] * 4
        + [pl.BlockSpec(memory_space=pl.ANY)] * 2
        + [vmem] * 2,
        out_specs=[vmem, vmem],
        out_shape=[f32(192, LANES), f32(8, LANES)],
        scratch_shapes=[
            pltpu.VMEM((16, 3, SIDE, 8, LANES), jnp.float32),
            pltpu.VMEM((256, 256), jnp.float32),
            pltpu.VMEM((256, 256), jnp.float32),
            pltpu.VMEM((256, 256), jnp.float32),
            pltpu.VMEM((16, 8, LANES), jnp.float32),
            pltpu.VMEM((5, SIDE, 8, LANES), jnp.float32),
            pltpu.SemaphoreType.DMA((2,)),
        ],
        compiler_params=params(),
    )(place, received, support_labels, target_labels, pack, *units, *planes)


def on_device(support, support_labels, targets, target_labels):
    tgt_id, sup_id = lax.axis_index("tgt"), lax.axis_index("sup")
    place = jnp.stack([tgt_id, sup_id]).astype(jnp.int32)
    image = support.reshape(24, LANES)
    label_row = jnp.zeros((8, LANES), jnp.float32)
    label_row = label_row.at[0, :32].set(target_labels.astype(jnp.float32))
    message = jnp.concatenate([image, label_row], axis=0)
    columns = lax.all_to_all(
        jnp.broadcast_to(message, (8, 32, LANES)), "tgt", 0, 0, tiled=True
    )
    rows = lax.all_to_all(
        jnp.broadcast_to(image.reshape(3, 8, LANES), (32, 3, 8, LANES)), "sup", 0, 0, tiled=True
    )
    all_labels = columns[:, 24, :32].reshape(1, 256).astype(jnp.int32)
    pack = column_pack(columns.reshape(256, LANES))
    entries_t, units_t, planes_t = pair_maps(
        place, targets.reshape(32, 3, 8, LANES), pack, False
    )
    entries_s, units_s, planes_s = pair_maps(place, rows, pack, True)
    payload = jnp.stack([entries_s[:, :32].reshape(2, LANES), entries_t[:, :32].reshape(2, LANES)])
    received = lax.all_to_all(
        jnp.broadcast_to(payload.reshape(4, LANES), (256, 4, LANES)), BOTH, 0, 0, tiled=True
    )
    partial, objective = solve_and_grad(
        place,
        received.reshape(1024, LANES),
        support_labels.reshape(1, 256),
        all_labels,
        pack,
        (units_t, units_s),
        (planes_t, planes_s),
    )
    pieces = lax.all_to_all(partial.reshape(8, 3, 8, LANES), "tgt", 0, 0, tiled=True)
    return jnp.sum(pieces, axis=0).reshape(1, 3, 1024), objective[0, 0]


def solution(mesh):
    placed = (P(BOTH, None, None), P(), P("tgt", None, None), P("tgt"))
    return jax.shard_map(
        on_device,
        mesh=mesh,
        in_specs=placed,
        out_specs=(P(BOTH, None, None), P()),
        check_vma=False,
    )
```

time: 1440 us -> 116 us (0.08)
  waiting for transfers between devices: 898 us -> 25.3 us
  other arithmetic: 268 us -> 3.41 us
  blocking collectives: 162 us -> 14.4 us
  local copies, waits for them, and re-layouts: 68.4 us -> 9.15 us
  Pallas kernels: 0 us -> 38.7 us
  starting transfers between devices: 0.33 us -> 23.4 us
  between operations: 19.3 us -> 0.68 us
    all_gather x2 -> x0, waiting for transfers between devices: 418 us -> none  [the longest x1 401 us: on_device(): gathered = lax.all_gather(support, ('tgt', 'sup'), axis=0, tiled=True)]
    unnamed x5 -> x0, waiting for transfers between devices: 262 us -> none
    psum x1 -> x0, waiting for transfers between devices: 218 us -> none  [on_device(): kernel_ss = lax.psum(placed + placed.T, ('tgt', 'sup'))]
    unnamed x2 -> x0, blocking collectives: 84.8 us -> none
    psum x1 -> x0, blocking collectives: 77.5 us -> none  [on_device(): lax.psum(jnp.dot(kernel_ts, coeff_own, precision=lax.Precision.HIGHEST),...]
    another operation x12 -> x3, other arithmetic: 74.3 us -> 1.32 us  [the longest x9 54.4 us: fit_coeffs(): jnp.linalg.cholesky(kernel + ridge * jnp.eye(kernel.shape[0], dtype=jnp.f...]
    reduce_sum x64 -> x1, other arithmetic: 72.2 us -> 0.61 us  [on_device(): return (jnp.sum(pieces, axis=0).reshape(1, 3, 1024), objective[0, 0])]
    mul x216 -> x0, other arithmetic: 40.4 us -> none  [the longest x24 11.8 us: ntk_block(): thetas = sigmas + 2.0 / 9.0 * stencil(slopes * thetas)]
  transfers between devices with their start and end apart: 4 -> 3, of which waited for: 4 -> 2; matrix products, arithmetic and copies ran while one was open for 6% -> 5% of each run, Pallas kernels for 0% -> 11%
where the time goes in v1:
time: 116 us; the launch traced here: 115 us
  Pallas kernels  38.7 us (33%)
  waiting for transfers between devices  25.3 us (22%)
  starting transfers between devices  23.4 us (20%)
  blocking collectives  14.4 us (12%)
  local copies, waits for them, and re-layouts  9.15 us (8%)
  other arithmetic  3.41 us (3%)
    pallas_call x2, Pallas kernels, pair_maps(): pl.pallas_call(functools.partial(maps_kernel, diagonal=diagonal), grid=(g...  21.3 us
    all_to_all x1, waiting for transfers between devices, on_device(): lax.all_to_all(jnp.broadcast_to(payload.reshape(4, LANES), (256, 4, LANES...  19.6 us
    pallas_call x1, Pallas kernels, solve_and_grad(): pl.pallas_call(solve_kernel, in_specs=[pl.BlockSpec(memory_space=pltpu.SM...  15.1 us
    all_to_all x1, blocking collectives, on_device(): lax.all_to_all(jnp.broadcast_to(message, (8, 32, LANES)), 'tgt', 0, 0, ti...  14.4 us
    all_to_all x1, starting transfers between devices, on_device(): lax.all_to_all(jnp.broadcast_to(image.reshape(3, 8, LANES), (32, 3, 8, LA...  10.8 us
    all_to_all x1, starting transfers between devices, on_device(): lax.all_to_all(jnp.broadcast_to(payload.reshape(4, LANES), (256, 4, LANES...  9.32 us
    all_to_all x1, waiting for transfers between devices, on_device(): lax.all_to_all(partial.reshape(8, 3, 8, LANES), 'tgt', 0, 0, tiled=True)  5.63 us
    all_to_all x1, starting transfers between devices, on_device(): lax.all_to_all(partial.reshape(8, 3, 8, LANES), 'tgt', 0, 0, tiled=True)  3.37 us
  transfers between devices with their start and end apart: 3, of which 2 were waited for; matrix products, arithmetic and copies ran while one was open for 5% of the time, Pallas kernels for 11%

profile of v1, /device:TPU:1, one launch (start us, length us, event | category | flops | bytes accessed | tf_op | source)
XLA Modules:
  0.0 115.1 jit_solution(17128734201356859489)
XLA Ops:
  0.6 0.7 convert_bitcast_fusion
  1.3 0.7 select_maximum_fusion
  2.0 14.4 %all_to_all.20 = f32[8,32,128]{2,1,0:T(8,128)} all-to-all(f32[8,32,128]{2,1,0:T(8,128)S(1)} %broadcast_in_dim.11), channel_id=1, replica_groups=mesh['tgt'=8,'sup'=32] {'tgt'}, dimensions={0} | all-to-all | bytes 262144 | tf_op jit(solution)/shard_map/all_to_all | solution.py:537
  16.4 1.5 %broadcast_in_dim.10 = f32[32,3,8,128]{3,2,1,0:T(8,128)} broadcast(f32[3,8,128]{2,1,0:T(8,128)} %bitcast.27), dimensions={1,2,3} | broadcast | bytes 405504 | tf_op jit(solution)/shard_map/broadcast_in_dim | solution.py:541
  17.9 10.8 %all-to-all-start = ((f32[32,3,8,128]{3,2,1,0:T(8,128)}), f32[32,3,8,128]{3,2,1,0:T(8,128)S(1)}, u32[]{:S(2)}, u32[]{:S(2)}) async-start(f32[32,3,8,128]{3,2,1,0:T(8,128)} %broadcast_in_dim.10), calls=%async_computation | async-start | bytes 786432 | tf_op jit(solution)/shard_map/all_to_all | solution.py:540
  28.7 1.1 copy.11
  29.8 0.8 copy.10.images_ref
  30.5 0.7 pad_add_fusion.place_ref
  31.2 2.3 %shard_map.59.pack_ref = f32[7,32,8,128]{3,2,1,0:T(8,128)} custom-call(f32[256,128]{1,0:T(8,128)} %bitcast.23), custom_call_target="tpu_custom_call" | custom-call | tf_op jit(solution)/shard_map/pallas_call | solution.py:472
  33.5 10.7 %shard_map.61 = (f32[8,128]{1,0:T(8,128)}, f32[8,3,32,8,128]{4,3,2,1,0:T(8,128)}, f32[8,3,4,8,128]{4,3,2,1,0:T(8,128)}) custom-call(s32[2]{0:T(128)} %pad_add_fusion.place_ref, f32[32,3,8,128]{3,2,1,0:T(8,128)} %copy.10.images_ref, f32[7,32,8,128]{3,2,1,0:T(8,128)} %shard_map.59.pack_ref), custom_call_target="tpu_custom_call" | custom-call | flops 36700160 | bytes 4194304 | tf_op jit(solution)/shard_map/pallas_call | solution.py:481
  44.1 0.8 stack_reshape.7
  44.9 0.8 copy-done.1
  45.7 10.6 %shard_map.60 = (f32[8,128]{1,0:T(8,128)}, f32[8,3,32,8,128]{4,3,2,1,0:T(8,128)}, f32[8,3,4,8,128]{4,3,2,1,0:T(8,128)}) custom-call(s32[2]{0:T(128)} %pad_add_fusion.place_ref, f32[32,3,8,128]{3,2,1,0:T(8,128)} %copy-done.1, f32[7,32,8,128]{3,2,1,0:T(8,128)} %shard_map.59.pack_ref), custom_call_target="tpu_custom_call" | custom-call | flops 36700160 | bytes 4194304 | tf_op jit(solution)/shard_map/pallas_call | solution.py:481
  56.3 0.8 stack_reshape.6
  57.1 0.9 broadcast_in_dim.12
  57.9 9.3 %all-to-all-start.2 = ((f32[256,4,128]{2,1,0:T(4,128)}), f32[256,4,128]{2,1,0:T(4,128)S(1)}, u32[]{:S(2)}, u32[]{:S(2)}) async-start(f32[256,4,128]{2,1,0:T(4,128)} %broadcast_in_dim.12), calls=%async_computation.2 | async-start | bytes 1048576 | tf_op jit(solution)/shard_map/all_to_all | solution.py:550
  67.3 0.8 fusion
  68.1 0.7 convert_element_type.10.target_labels_ref
  68.7 19.6 %all-to-all-done.2 = f32[256,4,128]{2,1,0:T(4,128)S(1)} async-done(((f32[256,4,128]{2,1,0:T(4,128)}), f32[256,4,128]{2,1,0:T(4,128)S(1)}, u32[]{:S(2)}, u32[]{:S(2)}) %all-to-all-start.2) | async-done | bytes 524320 | tf_op jit(solution)/shard_map/all_to_all | solution.py:550
  88.4 0.8 copy-done
  89.2 15.1 %shard_map.62 = (f32[192,128]{1,0:T(8,128)}, f32[8,128]{1,0:T(8,128)}) custom-call(s32[2]{0:T(128)} %pad_add_fusion.place_ref, f32[1024,128]{1,0:T(8,128)} %bitcast.21, s32[1,256]{1,0:T(1,128)} %bitcast.32, s32[1,256]{1,0:T(1,128)} %convert_element_type.10.target_labels_ref, f32[7,32,8,128]{3,2,1,0:T(8,128)} %shard_map.59.pack_ref, ...), custom_call_target="tpu_custom_call" | custom-call | tf_op jit(solution)/shard_map/pallas_call | solution.py:509
  104.3 3.4 %all-to-all-start.3 = ((f32[8,3,8,128]{3,2,1,0:T(8,128)}), f32[8,3,8,128]{3,2,1,0:T(8,128)S(1)}, u32[]{:S(2)}, u32[]{:S(2)}) async-start(f32[8,3,8,128]{3,2,1,0:T(8,128)} %bitcast.25), calls=%async_computation.3 | async-start | bytes 196608 | tf_op jit(solution)/shard_map/all_to_all | solution.py:562
  107.7 1.2 %slice.31 = f32[1,1]{1,0:T(1,128)} slice(f32[8,128]{1,0:T(8,128)} %get-tuple-element.29), slice={[0:1], [0:1]} | slice | bytes 8 | tf_op jit(solution)/shard_map/slice | solution.py:563
  108.9 5.6 %all-to-all-done.3 = f32[8,3,8,128]{3,2,1,0:T(8,128)S(1)} async-done(((f32[8,3,8,128]{3,2,1,0:T(8,128)}), f32[8,3,8,128]{3,2,1,0:T(8,128)S(1)}, u32[]{:S(2)}, u32[]{:S(2)}) %all-to-all-start.3) | async-done | bytes 98336 | tf_op jit(solution)/shard_map/all_to_all | solution.py:562
  (6 shorter events, 0.6 us)
Async XLA Ops:
  17.9 27.0 %all-to-all-start = ((f32[32,3,8,128]{3,2,1,0:T(8,128)}), f32[32,3,8,128]{3,2,1,0:T(8,128)S(1)}, u32[]{:S(2)}, u32[]{:S(2)}) async-start(f32[32,3,8,128]{3,2,1,0:T(8,128)} %broadcast_in_dim.10), calls=%async_computation | async-start | bytes 786432 | tf_op jit(solution)/shard_map/all_to_all | solution.py:540
  44.9 0.8 copy-start.1
  57.9 30.4 %all-to-all-start.2 = ((f32[256,4,128]{2,1,0:T(4,128)}), f32[256,4,128]{2,1,0:T(4,128)S(1)}, u32[]{:S(2)}, u32[]{:S(2)}) async-start(f32[256,4,128]{2,1,0:T(4,128)} %broadcast_in_dim.12), calls=%async_computation.2 | async-start | bytes 1048576 | tf_op jit(solution)/shard_map/all_to_all | solution.py:550
  88.4 0.8 copy-start
  104.3 10.2 %all-to-all-start.3 = ((f32[8,3,8,128]{3,2,1,0:T(8,128)}), f32[8,3,8,128]{3,2,1,0:T(8,128)S(1)}, u32[]{:S(2)}, u32[]{:S(2)}) async-start(f32[8,3,8,128]{3,2,1,0:T(8,128)} %bitcast.25), calls=%async_computation.3 | async-start | bytes 196608 | tf_op jit(solution)/shard_map/all_to_all | solution.py:562

commit v2 on v0

v2 whole, which is shorter than its diff:
```python
import functools
import math

import jax
import jax.numpy as jnp
from jax import lax
from jax.experimental import pallas as pl
from jax.experimental.pallas import tpu as pltpu
from jax.sharding import PartitionSpec as P

SIDE = 32
CLASSES = 10
BOTH = ("tgt", "sup")
LANES = 128
FOUR = 4
ALPHA1 = (2.0 / 9.0) / (2.0 * math.pi)
ALPHA2 = 1.0 / (2.0 * math.pi)
FIRST = 2.0 / 27.0
SECOND = 2.0 / 9.0
ACOS = (
    1.570796238860342,
    -0.21459108884050843,
    0.08883588680709523,
    -0.04919743925456755,
    0.027762915193263623,
    -0.01200339464235187,
    0.002611719889929782,
)
VMEM_LIMIT = 56 * 1024 * 1024
HIGHEST = lax.Precision.HIGHEST


def lane_index(shape):
    return lax.broadcasted_iota(jnp.int32, shape, len(shape) - 1)


def across(x, keep_left, keep_right):
    axis = x.ndim - 1
    return x + pltpu.roll(x, 1, axis) * keep_left + pltpu.roll(x, LANES - 1, axis) * keep_right


def edge_masks(shape):
    column = lane_index(shape) % SIDE
    return (column != 0).astype(jnp.float32), (column != SIDE - 1).astype(jnp.float32)


def swap_blocks(x0, x1, x2, x3):
    lane = lane_index(x0.shape)
    low = lane < 64
    even = (lane // SIDE) % 2 == 0
    axis = x0.ndim - 1
    a0 = jnp.where(low, x0, pltpu.roll(x2, 64, axis))
    a2 = jnp.where(low, pltpu.roll(x0, 64, axis), x2)
    a1 = jnp.where(low, x1, pltpu.roll(x3, 64, axis))
    a3 = jnp.where(low, pltpu.roll(x1, 64, axis), x3)
    y0 = jnp.where(even, a0, pltpu.roll(a1, 32, axis))
    y1 = jnp.where(even, pltpu.roll(a0, 96, axis), a1)
    y2 = jnp.where(even, a2, pltpu.roll(a3, 32, axis))
    y3 = jnp.where(even, pltpu.roll(a2, 96, axis), a3)
    return y0, y1, y2, y3


def spread_blocks(y):
    lane = lane_index(y.shape)
    low = lane < 64
    even = (lane // SIDE) % 2 == 0
    axis = y.ndim - 1
    turned = pltpu.roll(y, 64, axis)
    first = jnp.where(low, y, turned)
    last = jnp.where(low, turned, y)
    first_turned = pltpu.roll(first, 32, axis)
    last_turned = pltpu.roll(last, 32, axis)
    return (
        jnp.where(even, first, first_turned),
        jnp.where(even, first_turned, first),
        jnp.where(even, last, last_turned),
        jnp.where(even, last_turned, last),
    )


def message_kernel(image_ref, labels_ref, column_ref, row_ref):
    image = image_ref[...]
    hot = labels_ref[...].astype(jnp.float32)
    labels = jnp.broadcast_to(jnp.concatenate([hot] * FOUR, axis=1), (8, LANES))
    for d in range(8):
        column_ref[d, pl.ds(0, 24), :] = image
        column_ref[d, pl.ds(24, 8), :] = labels
    for d in range(row_ref.shape[0]):
        row_ref[d] = image


def column_maps(images_ref, pack_ref):
    keep_left, keep_right = edge_masks((8, LANES))
    for c in range(3):
        for s in range(8):
            y = images_ref[pl.ds(c * 8 + s, 8, stride=32), :]
            for k, z in enumerate(spread_blocks(y)):
                pack_ref[c, 4 * s + k] = z
    sums, variances = {}, {}
    for r in range(SIDE):
        b0, b1, b2 = pack_ref[0, r], pack_ref[1, r], pack_ref[2, r]
        sums[r] = across(b0 * b0 + b1 * b1 + b2 * b2, keep_left, keep_right)
    for r in range(SIDE):
        q = FIRST * vertical(sums, r) + 0.1
        inverse = lax.rsqrt(q)
        pack_ref[3, r] = inverse
        pack_ref[4, r] = q * inverse
        variances[r] = across(q, keep_left, keep_right)
    for r in range(SIDE):
        q = (0.5 * SECOND) * vertical(variances, r) + 0.1
        inverse = lax.rsqrt(q)
        pack_ref[5, r] = inverse
        pack_ref[6, r] = q * inverse


def row_maps(images, rows_ref):
    keep_left, keep_right = edge_masks((8, LANES))
    sublane = lax.broadcasted_iota(jnp.int32, (8, LANES), 0)

    def down(planes):
        above = jnp.where(sublane == 0, 0.0, pltpu.roll(planes[FOUR - 1], 1, 0))
        under = jnp.where(sublane == 7, 0.0, pltpu.roll(planes[0], 7, 0))
        line = [above, *planes, under]
        return [line[k] + line[k + 1] + line[k + 2] for k in range(FOUR)]

    squares = [0.0] * FOUR
    for c in range(3):
        planes = swap_blocks(*[images(i, c) for i in range(FOUR)])
        for k in range(FOUR):
            rows_ref[c, k] = FIRST * planes[k]
            squares[k] = squares[k] + planes[k] * planes[k]
    squares = [across(x, keep_left, keep_right) for x in squares]
    first = [FIRST * t + 0.1 for t in down(squares)]
    second = [
        (0.5 * SECOND) * t + 0.1 for t in down([across(q, keep_left, keep_right) for q in first])
    ]
    for k in range(FOUR):
        for n, q in ((3, first[k]), (5, second[k])):
            inverse = lax.rsqrt(q)
            rows_ref[n, k] = inverse
            rows_ref[n + 1, k] = q * inverse


def vertical(window, r):
    total = window[r]
    if r > 0:
        total = total + window[r - 1]
    if r < SIDE - 1:
        total = total + window[r + 1]
    return total


def vertical_pair(window, r, offset=None):
    both = window[r] + window[r + 1]
    if offset is not None:
        both = both + offset
    upper = both + window[r - 1] if r > 0 else both
    lower = both + window[r + 2] if r + 2 < SIDE else both
    return upper, lower


def arc(sigma, inverse, scale, alpha, bump):
    raw = sigma * inverse
    if bump is not None:
        raw = raw + bump
    cosine = jnp.clip(raw, -0.9999, 0.9999)
    inside = cosine == raw
    size = jnp.abs(cosine)
    below = 1.0 - size
    poly = jnp.float32(alpha * ACOS[-1])
    for coefficient in ACOS[-2::-1]:
        poly = poly * size + jnp.float32(alpha * coefficient)
    angle = (below * lax.rsqrt(below)) * poly
    slope = jnp.where(cosine >= 0.0, jnp.float32(alpha * math.pi) - angle, angle)
    rest = 1.0 - cosine * cosine
    root = alpha * lax.rsqrt(rest)
    value = scale * (rest * root + slope * cosine)
    return value, slope, root * inverse, inside


def group_maps(rows_ref, pack_ref, units_ref, bump):
    keep_left, keep_right = edge_masks((8, LANES))

    def row(c, r):
        return jnp.broadcast_to(rows_ref[c, r % FOUR, pl.ds(r // FOUR, 1), :], (8, LANES))

    cross, value_sum, slope_sum, dsig_sum, ds2_sum, dtheta_sum = {}, {}, {}, {}, {}, {}
    kept = {}
    total = jnp.zeros((8, LANES), jnp.float32)
    for step in range(0, SIDE + 10, 2):
        for r in (step, step + 1):
            if r < SIDE:
                x = sum(row(c, r) * pack_ref[c, r] for c in range(3))
                cross[r] = across(x, keep_left, keep_right)
        base = step - 2
        if 0 <= base < SIDE:
            for r, sigma in zip((base, base + 1), vertical_pair(cross, base, 0.1)):
                inverse = row(3, r) * pack_ref[3, r]
                scale = row(4, r) * pack_ref[4, r]
                value, slope, weight, inside = arc(sigma, inverse, scale, ALPHA1, None)
                value_sum[r] = across(value, keep_left, keep_right)
                slope_sum[r] = across(slope * sigma, keep_left, keep_right)
                if units_ref is not None:
                    kept[r] = (
                        sigma,
                        value,
                        slope,
                        jnp.where(inside, slope, 0.0),
                        jnp.where(inside, sigma * weight, 0.0),
                    )
        base = step - 4
        if 0 <= base < SIDE:
            for r, sigma, more in zip(
                (base, base + 1),
                vertical_pair(value_sum, base, 0.1),
                vertical_pair(slope_sum, base),
            ):
                theta = sigma + more
                inverse = row(5, r) * pack_ref[5, r]
                scale = row(6, r) * pack_ref[6, r]
                value, slope, weight, inside = arc(sigma, inverse, scale, ALPHA2, bump)
                total = total + (value + slope * theta)
                if units_ref is not None:
                    dsigma = jnp.where(inside, slope + theta * weight, 0.0)
                    units_ref[2, r] = value - dsigma * sigma
                    ds2_sum[r] = across(slope, keep_left, keep_right)
                    dsig_sum[r] = across(dsigma + slope, keep_left, keep_right)
        if units_ref is None:
            continue
        base = step - 6
        if 0 <= base < SIDE:
            for r, dvalue, dproduct in zip(
                (base, base + 1), vertical_pair(dsig_sum, base), vertical_pair(ds2_sum, base)
            ):
                sigma, value, slope, slope_in, weight_in = kept.pop(r)
                inner = slope_in * dvalue + dproduct * weight_in
                units_ref[1, r] = value * dvalue - inner * sigma
                dtheta_sum[r] = across(inner + dproduct * slope, keep_left, keep_right)
        base = step - 8
        if 0 <= base < SIDE:
            for r, unit in zip((base, base + 1), vertical_pair(dtheta_sum, base)):
                units_ref[0, r] = unit
    return total


def sum_entries(totals_ref):
    parts = [part.astype(jnp.float32) for part in split(totals_ref[...] * (2.0 / 1024.0), 3)]
    stacked = jnp.concatenate(parts + [jnp.zeros((8, 1024), jnp.float32)], axis=0)
    source = lax.broadcasted_iota(jnp.int32, (1024, LANES), 0) // SIDE
    pick = (source == lane_index((1024, LANES))).astype(jnp.bfloat16)
    sums = dot(stacked.astype(jnp.bfloat16), pick)
    return sums[:8] + (sums[8:16] + sums[16:24])


def keep_total(totals_ref, group, total):
    totals_ref[:, pl.ds(pl.multiple_of(group * LANES, LANES), LANES)] = total


def own_bump(group):
    image = group * FOUR + lane_index((8, LANES)) // SIDE
    column = lax.broadcasted_iota(jnp.int32, (8, LANES), 0)
    mine = lax.axis_index("sup") // 2
    own = jnp.logical_and(image == mine, column == lax.axis_index("tgt"))
    return own.astype(jnp.float32)


def copy_out(units_ref, units_hbm, sems, group):
    return pltpu.make_async_copy(units_ref.at[group], units_hbm.at[group], sems.at[group])


def row_kernel(images_ref, planes_ref):
    for group in range(8):

        def image(i, c, group=group):
            n = group * FOUR + i
            lines = [images_ref[c, pl.ds(n, 1), pl.ds(s * LANES, LANES)] for s in range(8)]
            return jnp.concatenate(lines, axis=0)

        row_maps(image, planes_ref.at[group])


def target_kernel(
    planes_ref, columns_ref, entries_ref, pack_ref, inverses_ref, units_hbm, units_ref, totals_ref, sems
):
    column_maps(columns_ref, pack_ref)
    block = lane_index((8, LANES)) // SIDE
    for n in range(2):
        for s in range(8):
            inverses_ref[n, s] = pick_blocks([pack_ref[3 + 2 * n, 4 * s + k] for k in range(FOUR)], block)

    def body(group, carry):
        keep_total(
            totals_ref,
            group,
            group_maps(planes_ref.at[group], pack_ref, units_ref.at[group], None),
        )
        copy_out(units_ref, units_hbm, sems, group).start()
        return carry

    lax.fori_loop(0, 8, body, 0)
    entries_ref[...] = sum_entries(totals_ref)
    for group in range(8):
        copy_out(units_ref, units_hbm, sems, group).wait()


def entries_kernel(
    own_ref, other_ref, pack_ref, entries_t_ref, payload_ref, planes_ref, totals_ref
):
    for half, images_ref in enumerate((own_ref, other_ref)):
        for group in range(FOUR):
            row_maps(
                lambda i, c: images_ref[group * FOUR + i, pl.ds(c * 8, 8), :],
                planes_ref.at[half * FOUR + group],
            )

    def body(group, carry):
        total = group_maps(planes_ref.at[group], pack_ref, None, own_bump(group))
        keep_total(totals_ref, group, total)
        return carry

    lax.fori_loop(0, 8, body, 0)
    entries = sum_entries(totals_ref)
    lane = lane_index((8, LANES))
    turned = jnp.where(lane < 16, pltpu.roll(entries, LANES - 16, 1), pltpu.roll(entries, 16, 1))
    turned = jnp.where(lane < SIDE, turned, 0.0)
    entries = jnp.where(lax.axis_index("sup") % 2 == 1, turned, entries)
    both = entries + pltpu.roll(entries_t_ref[...], SIDE, 1)
    both = both + pltpu.roll(pltpu.roll(both, 64, 1), FOUR, 0)
    for d in range(payload_ref.shape[0]):
        payload_ref[d] = both[:FOUR]


def units_kernel(planes_ref, pack_ref, units_hbm, units_ref, sems):
    def body(group, carry):
        group_maps(planes_ref.at[group], pack_ref, units_ref.at[group], own_bump(group))
        copy_out(units_ref, units_hbm, sems, group).start()
        return carry

    lax.fori_loop(0, 8, body, 0)
    for group in range(8):
        copy_out(units_ref, units_hbm, sems, group).wait()


def dot(a, b):
    return jnp.dot(a, b, preferred_element_type=jnp.float32)


def dot_nt(a, b):
    return lax.dot_general(a, b, (((1,), (1,)), ((), ())), preferred_element_type=jnp.float32)


def split(x, parts):
    result = []
    for _ in range(parts):
        result.append(x.astype(jnp.bfloat16))
        x = x - result[-1].astype(jnp.float32)
    return result


def product3(a, b):
    (ah, al), (bh, bl) = a, b
    return dot(ah, bh) + (dot(ah, bl) + dot(al, bh))


def thin_exact(a, b, product=dot):
    high, middle, low = split(a, 3)
    first = product(jnp.concatenate([high, middle, low], axis=0), b[0])
    second = product(jnp.concatenate([high, middle], axis=0), b[1])
    third = product(high, b[2])
    small = first[32:48] + second[16:32] + third
    return first[:16] + (first[16:32] + second[:16] + small)


def thin_near(a, b):
    high, middle = split(a, 2)
    first = dot(jnp.concatenate([high, middle], axis=0), b[0])
    return first[:16] + (first[16:] + dot(high, b[1]))


def pick_blocks(lines, block):
    low = jnp.where(block == 0, lines[0], lines[1])
    return jnp.where(block < 2, low, jnp.where(block == 2, lines[2], lines[3]))


def merge_blocks(lines, block):
    total = pick_blocks(lines, block)
    for d in range(1, FOUR):
        moved = pick_blocks([lines[(k - d) % FOUR] for k in range(FOUR)], block)
        total = total + pltpu.roll(moved, LANES - SIDE * d, 1)
    return total


def image_stencil(lines, masks, block):
    lines = [across(x, *masks) for x in lines]
    ups = [pltpu.roll(x, SIDE, 1) for x in lines]
    downs = [pltpu.roll(x, LANES - SIDE, 1) for x in lines]
    zero = jnp.zeros_like(lines[0])
    result = []
    for s in range(8):
        up = jnp.where(block == 0, ups[s - 1] if s else zero, ups[s])
        down = jnp.where(block == 3, downs[s + 1] if s < 7 else zero, downs[s])
        result.append(lines[s] + up + down)
    return result


def solve_kernel(
    own_hbm,
    other_hbm,
    support_labels_ref,
    columns_hbm,
    inverses_hbm,
    units_t_hbm,
    units_s_hbm,
    planes_t_hbm,
    planes_s_hbm,
    grad_ref,
    objective_ref,
    received_ref,
    columns_ref,
    inverses_ref,
    units_ref,
    planes_ref,
    kernel_ref,
    inverse_ref,
    matrix_parts,
    cross_parts,
    inverse_parts,
    weights_ref,
    grads_ref,
    sems,
):
    core = lax.axis_index("sup") % 2
    copies = [
        pltpu.make_async_copy(source, target, sems.at[n])
        for n, (source, target) in enumerate(
            [
                (own_hbm, received_ref.at[core]),
                (other_hbm, received_ref.at[1 - core]),
                (columns_hbm, columns_ref),
                (inverses_hbm, inverses_ref),
                (units_t_hbm, units_ref.at[pl.ds(0, 8)]),
                (units_s_hbm, units_ref.at[pl.ds(8, 8)]),
                (planes_t_hbm.at[:, pl.ds(0, 3)], planes_ref.at[pl.ds(0, 8)]),
                (planes_s_hbm.at[:, pl.ds(0, 3)], planes_ref.at[pl.ds(8, 8)]),
            ]
        )
    ]
    for copy in copies:
        copy.start()

    count = 256
    for copy in copies[:2]:
        copy.wait()
    for half in range(2):
        for j in range(FOUR):
            for h in range(2):
                blocks = []
                for i in range(FOUR):
                    start = (FOUR * h + i) * 16 * FOUR + j
                    blocks.append(received_ref[half, pl.ds(start, 16, stride=FOUR), :])
                for b, y in enumerate(swap_blocks(*blocks)):
                    rows = pl.ds((FOUR * (b // 2) + j) * 32 + 16 * half, 16)
                    lanes = pl.ds(h * LANES, LANES)
                    if b % 2 == 0:
                        kernel_ref[rows, lanes] = y
                    else:
                        for n, part in enumerate(split(y, 3)):
                            cross_parts[n, rows, lanes] = part

    matrix = kernel_ref[...]
    row_id = lax.broadcasted_iota(jnp.int32, (count, count), 0)
    col_id = lax.broadcasted_iota(jnp.int32, (count, count), 1)
    eye = row_id == col_id
    trace = jnp.sum(jnp.where(eye, matrix, 0.0))
    ridge = 0.1 * trace / count
    matrix = matrix + jnp.where(eye, ridge, 0.0)
    bound = jnp.max(jnp.sum(jnp.abs(matrix), axis=0, keepdims=True))
    spread = (bound - ridge) / (bound + ridge)
    start = 2.0 / (bound + ridge)
    square = spread * spread
    gain = 2.0 / (2.0 - square)
    inverse_ref[...] = (gain * start) * (jnp.where(eye, 2.0, 0.0) - start * matrix)
    for n, part in enumerate(split(matrix, 3)):
        matrix_parts[n] = part

    def improve(delta):
        square = delta * delta
        gain = 2.0 / (2.0 - square)
        x = inverse_ref[...]
        parts = split(x, 2)
        error = jnp.where(eye, 1.0, 0.0) - product3((matrix_parts[0], matrix_parts[1]), parts)
        inverse_ref[...] = gain * (x + product3(parts, split(error, 2)))
        return square / (2.0 - square)

    lax.while_loop(lambda delta: delta > 3e-3, improve, square / (2.0 - square))
    for n, part in enumerate(split(inverse_ref[...], 2)):
        inverse_parts[n] = part

    def solve(right):
        def refine(state):
            guess, _, rounds = state
            rest = right - thin_exact(guess, matrix_parts)
            step = thin_near(rest, inverse_parts)
            guess = guess + step
            return guess, jnp.sum(step * step) / jnp.sum(guess * guess), rounds + 1

        def going(state):
            return jnp.logical_and(state[1] > 1e-9, state[2] < 40)

        return lax.while_loop(going, refine, (thin_near(right, inverse_parts), 1.0, 0))[0]

    class_id = lax.broadcasted_iota(jnp.int32, (16, count), 0)

    def one_hot(labels):
        hot = (class_id == labels).astype(jnp.float32) - 0.1
        return jnp.where(class_id < CLASSES, hot, 0.0)

    coeffs = solve(one_hot(support_labels_ref[...]))
    for copy in copies[2:4]:
        copy.wait()
    lane1 = lane_index((1, LANES))
    halves = []
    for h in range(2):
        line = [columns_ref[pl.ds((FOUR * h + i) * 32 + 24, 1), :] for i in range(FOUR)]
        line = [jnp.where(lane1 // SIDE == i, x, 0.0) for i, x in enumerate(line)]
        halves.append((line[0] + line[1]) + (line[2] + line[3]))
    target_labels = jnp.concatenate(halves, axis=1).astype(jnp.int32)
    residual = thin_exact(coeffs, cross_parts) - one_hot(target_labels)
    objective_ref[...] = jnp.full((8, LANES), 0.5 * jnp.sum(residual * residual), jnp.float32)
    adjoint = solve(thin_exact(residual, cross_parts, dot_nt))
    trace_grad = -jnp.sum(adjoint * coeffs)

    mine_t = lax.axis_index("tgt")
    mine = core * 16 + lax.axis_index("sup") // 2
    coeff_parts, adjoint_parts = split(coeffs, 3), split(adjoint, 3)
    ids = lax.broadcasted_iota(jnp.int32, (16, count), 1)
    wanted = lax.broadcasted_iota(jnp.int32, (16, count), 0) * 32 + mine
    picked = dot_nt(
        (ids == wanted).astype(jnp.bfloat16), jnp.concatenate(coeff_parts + adjoint_parts, axis=0)
    ).astype(jnp.bfloat16)
    turn = lax.rem(count - 32 * mine_t, count)

    def row_parts(x):
        return split(pltpu.roll(x, turn, 1)[:, :LANES], 3)

    zero = jnp.zeros((48, LANES), jnp.bfloat16)
    pairs = 0.0
    for c, a, r in zip(row_parts(-coeffs), row_parts(-adjoint), row_parts(residual)):
        side_s = jnp.concatenate([a, a, a, c, c, c], axis=0)
        side_t = jnp.concatenate([r, r, r, zero], axis=0)
        pairs = pairs + dot(picked, jnp.concatenate([side_s, side_t], axis=1))
    sub8 = lax.broadcasted_iota(jnp.int32, (8, LANES), 0)
    lane8 = lane_index((8, LANES))
    own = jnp.logical_and(sub8 == mine_t, lane8 == mine)
    pairs_s = pairs[:8, :LANES] + jnp.where(own, (0.2 / count) * trace_grad, 0.0)
    pairs = jnp.concatenate([pairs[:8, LANES:], pairs_s], axis=0)
    pairs = jnp.where(lane_index((16, LANES)) < SIDE, pairs * (2.0 / 1024.0), 0.0)
    high, middle, low = [part.astype(jnp.float32) for part in split(pairs, 3)]
    stacked = high + pltpu.roll(middle, 32, 1) + pltpu.roll(low, 64, 1)
    widen = lax.broadcasted_iota(jnp.int32, (LANES, 1024), 0) % SIDE
    widen = widen == lax.broadcasted_iota(jnp.int32, (LANES, 1024), 1) // SIDE
    wide = dot(stacked.astype(jnp.bfloat16), widen.astype(jnp.bfloat16))
    for g in range(8):
        weights_ref[g] = wide[:8, g * LANES : (g + 1) * LANES]
        weights_ref[8 + lax.rem(g + FOUR * core, 8)] = wide[8:, g * LANES : (g + 1) * LANES]

    for copy in copies[4:]:
        copy.wait()

    block = lane8 // SIDE

    def gather_line(s, carry):
        lines = [[] for _ in range(5)]
        for k in range(FOUR):
            r = s * FOUR + k
            sums = [None] * 5
            for g in range(16):
                weight = weights_ref[g]
                dx = weight * units_ref[g, 0, r]
                terms = [
                    dx * jnp.broadcast_to(planes_ref[g, c, k, pl.ds(s, 1), :], (8, LANES))
                    for c in range(3)
                ]
                terms.append(weight * units_ref[g, 1, r])
                terms.append(weight * units_ref[g, 2, r])
                sums = [t if a is None else a + t for a, t in zip(sums, terms)]
            for n in range(5):
                lines[n].append(sums[n])
        for n in range(5):
            grads_ref[n, s] = merge_blocks(lines[n], block)
        return carry

    lax.fori_loop(0, 8, gather_line, 0, unroll=2)

    masks = edge_masks((8, LANES))
    second = [0.5 * inverses_ref[1, s] * inverses_ref[1, s] * grads_ref[4, s] for s in range(8)]
    second = image_stencil(second, masks, block)
    first = [
        0.5 * inverses_ref[0, s] * inverses_ref[0, s] * grads_ref[3, s] + (0.5 * SECOND) * second[s]
        for s in range(8)
    ]
    first = image_stencil(first, masks, block)
    for s in range(8):
        for c in range(3):
            image = columns_ref[pl.ds(c * 8 + s, 8, stride=32), :]
            grad_ref[pl.ds(c * 8 + s, 8, stride=24), :] = (
                grads_ref[c, s] + (2.0 * FIRST) * first[s] * image
            )


def f32(*shape):
    return jax.ShapeDtypeStruct(shape, jnp.float32)


HBM = pl.BlockSpec(memory_space=pl.ANY)
VMEM = pl.BlockSpec(memory_space=pltpu.VMEM)


def call(kernel, ins, outs, shapes, scratch, work=0):
    return pl.pallas_call(
        kernel,
        in_specs=ins,
        out_specs=outs,
        out_shape=shapes,
        scratch_shapes=scratch,
        compiler_params=pltpu.CompilerParams(vmem_limit_bytes=VMEM_LIMIT),
        cost_estimate=pl.CostEstimate(flops=work, bytes_accessed=4 << 20, transcendentals=0),
    )


PLANES = (8, 7, FOUR, 8, LANES)
UNITS = (8, 3, SIDE, 8, LANES)
PACK = (7, SIDE, 8, LANES)
WORK = 256 * 1024 * 140


def on_device(support, support_labels, targets, target_labels):
    scratch = pltpu.VMEM
    zx = [[2 * m + core for m in range(16)] for core in range(2)]
    chips = [[2 * chip + core for chip in range(128)] for core in range(2)]
    cores = [(device, device ^ 1) for device in range(32)]

    column_message, row_message = call(
        message_kernel, [VMEM] * 2, [VMEM] * 2, [f32(8, 32, LANES), f32(16, 24, LANES)], []
    )(support.reshape(24, LANES), target_labels.reshape(1, 32))
    columns = lax.all_to_all(column_message, "tgt", 0, 0, tiled=True).reshape(256, LANES)
    planes_t = call(row_kernel, [VMEM], VMEM, f32(*PLANES), [], WORK // 2)(
        targets.transpose(1, 0, 2)
    )
    labels = support_labels.reshape(8, 16, 2).transpose(0, 2, 1).reshape(1, 256)
    columns, planes_t, row_message, labels = lax.optimization_barrier(
        (columns, planes_t, row_message, labels)
    )
    rows = lax.all_to_all(row_message, "sup", 0, 0, tiled=True, axis_index_groups=zx)
    entries_t, pack, inverses, units_t = call(
        target_kernel,
        [VMEM] * 2,
        [VMEM] * 3 + [HBM],
        [f32(8, LANES), f32(*PACK), f32(2, 8, 8, LANES), f32(*UNITS)],
        [
            scratch(UNITS, jnp.float32),
            scratch((8, 1024), jnp.float32),
            pltpu.SemaphoreType.DMA((8,)),
        ],
        WORK,
    )(planes_t, columns)
    rows, entries_t = lax.optimization_barrier((rows, entries_t))
    rows_other = lax.ppermute(rows, "sup", cores)
    payload, planes_s = call(
        entries_kernel,
        [VMEM] * 4,
        [VMEM] * 2,
        [f32(128, FOUR, LANES), f32(*PLANES)],
        [scratch((8, 1024), jnp.float32)],
        WORK // 2,
    )(rows, rows_other, pack, entries_t)
    received = lax.all_to_all(payload, BOTH, 0, 0, tiled=True, axis_index_groups=chips)
    units_s = call(
        units_kernel,
        [VMEM] * 2,
        HBM,
        f32(*UNITS),
        [scratch(UNITS, jnp.float32), pltpu.SemaphoreType.DMA((8,))],
        WORK,
    )(planes_s, pack)
    received, units_s = lax.optimization_barrier((received, units_s))
    received_other = lax.ppermute(received, "sup", cores)
    partial, objective = call(
        solve_kernel,
        [HBM] * 2 + [VMEM] + [HBM] * 6,
        [VMEM] * 2,
        [f32(192, LANES), f32(8, LANES)],
        [
            scratch((2, 512, LANES), jnp.float32),
            scratch((256, LANES), jnp.float32),
            scratch((2, 8, 8, LANES), jnp.float32),
            scratch((16, 3, SIDE, 8, LANES), jnp.float32),
            scratch((16, 3, FOUR, 8, LANES), jnp.float32),
            scratch((256, 256), jnp.float32),
            scratch((256, 256), jnp.float32),
            scratch((3, 256, 256), jnp.bfloat16),
            scratch((3, 256, 256), jnp.bfloat16),
            scratch((2, 256, 256), jnp.bfloat16),
            scratch((16, 8, LANES), jnp.float32),
            scratch((5, 8, 8, LANES), jnp.float32),
            pltpu.SemaphoreType.DMA((8,)),
        ],
        WORK,
    )(
        received.reshape(512, LANES),
        received_other.reshape(512, LANES),
        labels,
        columns,
        inverses,
        units_t,
        units_s,
        planes_t,
        planes_s,
    )
    pieces = lax.all_to_all(partial.reshape(8, 24, LANES), "tgt", 0, 0, tiled=True)
    return jnp.sum(pieces, axis=0).reshape(1, 3, 1024), objective[0, 0]


def solution(mesh):
    placed = (P(BOTH, None, None), P(), P("tgt", None, None), P("tgt"))
    return jax.shard_map(
        on_device,
        mesh=mesh,
        in_specs=placed,
        out_specs=(P(BOTH, None, None), P()),
        check_vma=False,
    )
```

time: 1440 us -> 99.4 us (0.07)
  waiting for transfers between devices: 898 us -> 14.6 us
  other arithmetic: 268 us -> 0.61 us
  blocking collectives: 162 us -> 0 us
  local copies, waits for them, and re-layouts: 68.4 us -> 4.2 us
  Pallas kernels: 0 us -> 43.5 us
  starting transfers between devices: 0.33 us -> 35.1 us
  between operations: 19.3 us -> 0.72 us
    all_gather x2 -> x0, waiting for transfers between devices: 418 us -> none  [the longest x1 401 us: on_device(): gathered = lax.all_gather(support, ('tgt', 'sup'), axis=0, tiled=True)]
    unnamed x5 -> x0, waiting for transfers between devices: 262 us -> none
    psum x1 -> x0, waiting for transfers between devices: 218 us -> none  [on_device(): kernel_ss = lax.psum(placed + placed.T, ('tgt', 'sup'))]
    unnamed x2 -> x0, blocking collectives: 84.8 us -> none
    psum x1 -> x0, blocking collectives: 77.5 us -> none  [on_device(): lax.psum(jnp.dot(kernel_ts, coeff_own, precision=lax.Precision.HIGHEST),...]
    another operation x12 -> x0, other arithmetic: 74.3 us -> none  [the longest x9 54.4 us: fit_coeffs(): jnp.linalg.cholesky(kernel + ridge * jnp.eye(kernel.shape[0], dtype=jnp.f...]
    reduce_sum x64 -> x1, other arithmetic: 72.2 us -> 0.61 us  [on_device(): return (jnp.sum(pieces, axis=0).reshape(1, 3, 1024), objective[0, 0])]
    pallas_call x0 -> x6, Pallas kernels: none -> 43.5 us  [the longest x1 12.3 us: on_device(): call(solve_kernel, [HBM] * 2 + [VMEM] + [HBM] * 6, [VMEM] * 2, [f32(192,...]
  transfers between devices with their start and end apart: 4 -> 6, of which waited for: 4 -> 5; matrix products, arithmetic and copies ran while one was open for 6% -> 3% of each run, Pallas kernels for 0% -> 23%
where the time goes in v2:
time: 99.4 us; the launch traced here: 98.8 us
  Pallas kernels  43.5 us (44%)
  starting transfers between devices  35.1 us (35%)
  waiting for transfers between devices  14.6 us (15%)
  local copies, waits for them, and re-layouts  4.2 us (4%)
    pallas_call x1, Pallas kernels, on_device(): call(solve_kernel, [HBM] * 2 + [VMEM] + [HBM] * 6, [VMEM] * 2, [f32(192,...  12.3 us
    all_to_all x1, starting transfers between devices, on_device(): lax.all_to_all(payload, BOTH, 0, 0, tiled=True, axis_index_groups=chips)  11.2 us
    pallas_call x1, Pallas kernels, on_device(): call(target_kernel, [VMEM] * 2, [VMEM] * 3 + [HBM], [f32(8, LANES), f32(*...  10.7 us
    pallas_call x1, Pallas kernels, on_device(): call(units_kernel, [VMEM] * 2, HBM, f32(*UNITS), [scratch(UNITS, jnp.floa...  9.2 us
    all_to_all x1, starting transfers between devices, on_device(): lax.all_to_all(row_message, 'sup', 0, 0, tiled=True, axis_index_groups=zx)  8.32 us
    all_to_all x1, starting transfers between devices, on_device(): lax.all_to_all(column_message, 'tgt', 0, 0, tiled=True).reshape(256, LANES)  7.48 us
    pallas_call x1, Pallas kernels, on_device(): call(entries_kernel, [VMEM] * 4, [VMEM] * 2, [f32(128, FOUR, LANES), f32(...  7.13 us
    all_to_all x1, waiting for transfers between devices, on_device(): lax.all_to_all(partial.reshape(8, 24, LANES), 'tgt', 0, 0, tiled=True)  5.63 us
  transfers between devices with their start and end apart: 6, of which 5 were waited for; matrix products, arithmetic and copies ran while one was open for 3% of the time, Pallas kernels for 23%

profile of v2, /device:TPU:1, one launch (start us, length us, event | category | flops | bytes accessed | tf_op | source)
XLA Modules:
  0.0 98.8 jit_solution(7973420126847422147)
XLA Ops:
  0.6 1.5 %shard_map.59 = (f32[8,32,128]{2,1,0:T(8,128)}, f32[16,24,128]{2,1,0:T(8,128)}) custom-call(f32[24,128]{1,0:T(8,128)} %bitcast.18, s32[1,32]{1,0:T(1,128)} %bitcast.19), custom_call_target="tpu_custom_call" | custom-call | bytes 4194304 | tf_op jit(solution)/shard_map/pallas_call | solution.py:643
  2.1 7.5 %all-to-all-start = ((f32[8,32,128]{2,1,0:T(8,128)}), f32[8,32,128]{2,1,0:T(8,128)S(1)}, u32[]{:S(2)}, u32[]{:S(2)}) async-start(f32[8,32,128]{2,1,0:T(8,128)} %get-tuple-element.20), calls=%async_computation | async-start | bytes 262144 | tf_op jit(solution)/shard_map/all_to_all | solution.py:646
  9.6 0.8 reshape.34
  10.4 0.1 copy.6
  10.5 0.7 reshape.35.support_labels_ref
  11.2 2.8 %shard_map.60.planes_ref.planes_t_hbm = f32[8,7,4,8,128]{4,3,2,1,0:T(8,128)} custom-call(f32[3,32,1024]{2,1,0:T(8,128)} %bitcast.13), custom_call_target="tpu_custom_call" | custom-call | flops 18350080 | bytes 4194304 | tf_op jit(solution)/shard_map/pallas_call | solution.py:647
  14.0 2.7 %all-to-all-done = f32[8,32,128]{2,1,0:T(8,128)S(1)} async-done(((f32[8,32,128]{2,1,0:T(8,128)}), f32[8,32,128]{2,1,0:T(8,128)S(1)}, u32[]{:S(2)}, u32[]{:S(2)}) %all-to-all-start) | async-done | bytes 131104 | tf_op jit(solution)/shard_map/all_to_all | solution.py:646
  16.6 8.3 %all-to-all-start.1 = ((f32[16,24,128]{2,1,0:T(8,128)}), f32[16,24,128]{2,1,0:T(8,128)S(1)}, u32[]{:S(2)}, u32[]{:S(2)}) async-start(f32[16,24,128]{2,1,0:T(8,128)} %get-tuple-element.22), calls=%async_computation.1 | async-start | bytes 393216 | tf_op jit(solution)/shard_map/all_to_all | solution.py:654
  25.0 10.7 %shard_map.61 = (f32[8,128]{1,0:T(8,128)}, f32[7,32,8,128]{3,2,1,0:T(8,128)}, f32[2,8,8,128]{3,2,1,0:T(8,128)}, f32[8,3,32,8,128]{4,3,2,1,0:T(8,128)}) custom-call(f32[8,7,4,8,128]{4,3,2,1,0:T(8,128)} %shard_map.60.planes_ref.planes_t_hbm, f32[256,128]{1,0:T(8,128)} %bitcast.10), custom_call_target="tpu_custom_call" | custom-call | flops 36700160 | bytes 4194304 | tf_op jit(solution)/shard_map/pallas_call | solution.py:655
  35.7 2.5 %collective-permute-start = (f32[16,24,128]{2,1,0:T(8,128)S(1)}, f32[16,24,128]{2,1,0:T(8,128)S(1)}, u32[]{:S(2)}, u32[]{:S(2)}) collective-permute-start(f32[16,24,128]{2,1,0:T(8,128)S(1)} %all-to-all-done.1.own_ref), channel_id=1, source_target_pairs={{0,1},{1,0},{2,3},{3,2},{4,5},{5,4},{6,7},{7,6},{8,9},{9,8},{10,11... | collective-permute-start | bytes 589832 | tf_op jit(solution)/shard_map/ppermute | solution.py:668
  38.1 1.1 %collective-permute-done.other_ref = f32[16,24,128]{2,1,0:T(8,128)S(1)} collective-permute-done((f32[16,24,128]{2,1,0:T(8,128)S(1)}, f32[16,24,128]{2,1,0:T(8,128)S(1)}, u32[]{:S(2)}, u32[]{:S(2)}) %collective-permute-start) | collective-permute-done | bytes 196640 | tf_op jit(solution)/shard_map/ppermute | solution.py:668
  39.2 0.7 copy-done.4
  39.9 7.1 %shard_map.62 = (f32[128,4,128]{2,1,0:T(4,128)}, f32[8,7,4,8,128]{4,3,2,1,0:T(8,128)}) custom-call(f32[16,24,128]{2,1,0:T(8,128)} %copy-done.2, f32[16,24,128]{2,1,0:T(8,128)} %copy-done.4, f32[7,32,8,128]{3,2,1,0:T(8,128)} %get-tuple-element.27.pack_ref, f32[8,128]{1,0:T(8,128)} %get-tuple-element.28.entries_t_ref), custom_call_target="tpu_custom_call" | custom-call | flops 18350080 | bytes 4194304 | tf_op jit(solution)/shard_map/pallas_call | solution.py:669
  47.0 11.2 %all-to-all-start.2 = ((f32[128,4,128]{2,1,0:T(4,128)}), f32[128,4,128]{2,1,0:T(4,128)S(1)}, u32[]{:S(2)}, u32[]{:S(2)}) async-start(f32[128,4,128]{2,1,0:T(4,128)} %get-tuple-element.29), calls=%async_computation.2 | async-start | bytes 524288 | tf_op jit(solution)/shard_map/all_to_all | solution.py:677
  58.2 9.2 %shard_map.63.units_s_hbm = f32[8,3,32,8,128]{4,3,2,1,0:T(8,128)} custom-call(f32[8,7,4,8,128]{4,3,2,1,0:T(8,128)} %get-tuple-element.30.planes_ref.planes_s_hbm, f32[7,32,8,128]{3,2,1,0:T(8,128)} %get-tuple-element.27.pack_ref), custom_call_target="tpu_custom_call" | custom-call | flops 36700160 | bytes 4194304 | tf_op jit(solution)/shard_map/pallas_call | solution.py:678
  67.5 4.1 %all-to-all-done.2 = f32[128,4,128]{2,1,0:T(4,128)S(1)} async-done(((f32[128,4,128]{2,1,0:T(4,128)}), f32[128,4,128]{2,1,0:T(4,128)S(1)}, u32[]{:S(2)}, u32[]{:S(2)}) %all-to-all-start.2) | async-done | bytes 262176 | tf_op jit(solution)/shard_map/all_to_all | solution.py:677
  71.5 2.3 %collective-permute-start.1 = (f32[128,4,128]{2,1,0:T(4,128)S(1)}, f32[128,4,128]{2,1,0:T(4,128)S(1)}, u32[]{:S(2)}, u32[]{:S(2)}) collective-permute-start(f32[128,4,128]{2,1,0:T(4,128)S(1)} %all-to-all-done.2), channel_id=1, source_target_pairs={{0,1},{1,0},{2,3},{3,2},{4,5},{5,4},{6,7},{7,6},{8,9},{9,8},{10,11... | collective-permute-start | bytes 786440 | tf_op jit(solution)/shard_map/ppermute | solution.py:687
  73.8 1.2 %collective-permute-done.1 = f32[128,4,128]{2,1,0:T(4,128)S(1)} collective-permute-done((f32[128,4,128]{2,1,0:T(4,128)S(1)}, f32[128,4,128]{2,1,0:T(4,128)S(1)}, u32[]{:S(2)}, u32[]{:S(2)}) %collective-permute-start.1) | collective-permute-done | bytes 262176 | tf_op jit(solution)/shard_map/ppermute | solution.py:687
  75.0 0.7 copy-done.3
  75.7 12.3 %shard_map.64 = (f32[192,128]{1,0:T(8,128)}, f32[8,128]{1,0:T(8,128)}) custom-call(f32[512,128]{1,0:T(8,128)} %bitcast.12, f32[512,128]{1,0:T(8,128)} %bitcast.14, s32[1,256]{1,0:T(1,128)} %reshape.35.support_labels_ref, f32[256,128]{1,0:T(8,128)} %bitcast.11, f32[2,8,8,128]{3,2,1,0:T(8,128)} %get-tuple-element.33.inverses_hbm, ...), custom_call_target="tpu_custom_call" | custom-call | flops 36700160 | bytes 4194304 | tf_op jit(solution)/shard_map/pallas_call | solution.py:688
  87.9 3.4 %all-to-all-start.3 = ((f32[8,24,128]{2,1,0:T(8,128)}), f32[8,24,128]{2,1,0:T(8,128)S(1)}, u32[]{:S(2)}, u32[]{:S(2)}) async-start(f32[8,24,128]{2,1,0:T(8,128)} %bitcast.16), calls=%async_computation.3 | async-start | bytes 196608 | tf_op jit(solution)/shard_map/all_to_all | solution.py:720
  91.3 1.2 %slice.3 = f32[1,1]{1,0:T(1,128)} slice(f32[8,128]{1,0:T(8,128)} %get-tuple-element.37), slice={[0:1], [0:1]} | slice | bytes 8 | tf_op jit(solution)/shard_map/slice | solution.py:721
  92.5 5.6 %all-to-all-done.3 = f32[8,24,128]{2,1,0:T(8,128)S(1)} async-done(((f32[8,24,128]{2,1,0:T(8,128)}), f32[8,24,128]{2,1,0:T(8,128)S(1)}, u32[]{:S(2)}, u32[]{:S(2)}) %all-to-all-start.3) | async-done | bytes 98336 | tf_op jit(solution)/shard_map/all_to_all | solution.py:720
  98.2 0.6 reduce_sum.9
  (9 shorter events, 0.0 us)
Async XLA Ops:
  2.1 14.5 %all-to-all-start = ((f32[8,32,128]{2,1,0:T(8,128)}), f32[8,32,128]{2,1,0:T(8,128)S(1)}, u32[]{:S(2)}, u32[]{:S(2)}) async-start(f32[8,32,128]{2,1,0:T(8,128)} %get-tuple-element.20), calls=%async_computation | async-start | bytes 262144 | tf_op jit(solution)/shard_map/all_to_all | solution.py:646
  16.6 8.3 %copy-start = (f32[8,32,128]{2,1,0:T(8,128)}, f32[8,32,128]{2,1,0:T(8,128)S(1)}, u32[]{:S(2)}) copy-start(f32[8,32,128]{2,1,0:T(8,128)S(1)} %all-to-all-done) | copy-start | bytes 393220
  16.6 19.0 %all-to-all-start.1 = ((f32[16,24,128]{2,1,0:T(8,128)}), f32[16,24,128]{2,1,0:T(8,128)S(1)}, u32[]{:S(2)}, u32[]{:S(2)}) async-start(f32[16,24,128]{2,1,0:T(8,128)} %get-tuple-element.22), calls=%async_computation.1 | async-start | bytes 393216 | tf_op jit(solution)/shard_map/all_to_all | solution.py:654
  35.7 3.6 %copy-start.2 = (f32[16,24,128]{2,1,0:T(8,128)}, f32[16,24,128]{2,1,0:T(8,128)S(1)}, u32[]{:S(2)}) copy-start(f32[16,24,128]{2,1,0:T(8,128)S(1)} %all-to-all-done.1.own_ref) | copy-start | bytes 589828
  35.7 3.5 %collective-permute-start = (f32[16,24,128]{2,1,0:T(8,128)S(1)}, f32[16,24,128]{2,1,0:T(8,128)S(1)}, u32[]{:S(2)}, u32[]{:S(2)}) collective-permute-start(f32[16,24,128]{2,1,0:T(8,128)S(1)} %all-to-all-done.1.own_ref), channel_id=1, source_target_pairs={{0,1},{1,0},{2,3},{3,2},{4,5},{5,4},{6,7},{7,6},{8,9},{9,8},{10,11... | collective-permute-start | bytes 589832 | tf_op jit(solution)/shard_map/ppermute | solution.py:668
  39.2 0.7 copy-start.4
  47.0 24.5 %all-to-all-start.2 = ((f32[128,4,128]{2,1,0:T(4,128)}), f32[128,4,128]{2,1,0:T(4,128)S(1)}, u32[]{:S(2)}, u32[]{:S(2)}) async-start(f32[128,4,128]{2,1,0:T(4,128)} %get-tuple-element.29), calls=%async_computation.2 | async-start | bytes 524288 | tf_op jit(solution)/shard_map/all_to_all | solution.py:677
  71.5 3.5 %copy-start.1 = (f32[128,4,128]{2,1,0:T(4,128)}, f32[128,4,128]{2,1,0:T(4,128)S(1)}, u32[]{:S(2)}) copy-start(f32[128,4,128]{2,1,0:T(4,128)S(1)} %all-to-all-done.2) | copy-start | bytes 786436
  71.5 3.4 %collective-permute-start.1 = (f32[128,4,128]{2,1,0:T(4,128)S(1)}, f32[128,4,128]{2,1,0:T(4,128)S(1)}, u32[]{:S(2)}, u32[]{:S(2)}) collective-permute-start(f32[128,4,128]{2,1,0:T(4,128)S(1)} %all-to-all-done.2), channel_id=1, source_target_pairs={{0,1},{1,0},{2,3},{3,2},{4,5},{5,4},{6,7},{7,6},{8,9},{9,8},{10,11... | collective-permute-start | bytes 786440 | tf_op jit(solution)/shard_map/ppermute | solution.py:687
  75.0 0.7 copy-start.3
  87.9 10.2 %all-to-all-start.3 = ((f32[8,24,128]{2,1,0:T(8,128)}), f32[8,24,128]{2,1,0:T(8,128)S(1)}, u32[]{:S(2)}, u32[]{:S(2)}) async-start(f32[8,24,128]{2,1,0:T(8,128)} %bitcast.16), calls=%async_computation.3 | async-start | bytes 196608 | tf_op jit(solution)/shard_map/all_to_all | solution.py:720

commit v3 on v2

--- a/solution.py
+++ b/solution.py
@@ -12,6 +12,7 @@
 CLASSES = 10
 BOTH = ("tgt", "sup")
 LANES = 128
+MAPS = 7 * 32
 FOUR = 4
 ALPHA1 = (2.0 / 9.0) / (2.0 * math.pi)
 ALPHA2 = 1.0 / (2.0 * math.pi)
@@ -26,7 +27,7 @@
     -0.01200339464235187,
     0.002611719889929782,
 )
-VMEM_LIMIT = 56 * 1024 * 1024
+KIB = 1024
 HIGHEST = lax.Precision.HIGHEST
 
 
@@ -44,20 +45,18 @@
     return (column != 0).astype(jnp.float32), (column != SIDE - 1).astype(jnp.float32)
 
 
-def swap_blocks(x0, x1, x2, x3):
-    lane = lane_index(x0.shape)
-    low = lane < 64
-    even = (lane // SIDE) % 2 == 0
-    axis = x0.ndim - 1
-    a0 = jnp.where(low, x0, pltpu.roll(x2, 64, axis))
-    a2 = jnp.where(low, pltpu.roll(x0, 64, axis), x2)
-    a1 = jnp.where(low, x1, pltpu.roll(x3, 64, axis))
-    a3 = jnp.where(low, pltpu.roll(x1, 64, axis), x3)
-    y0 = jnp.where(even, a0, pltpu.roll(a1, 32, axis))
-    y1 = jnp.where(even, pltpu.roll(a0, 96, axis), a1)
-    y2 = jnp.where(even, a2, pltpu.roll(a3, 32, axis))
-    y3 = jnp.where(even, pltpu.roll(a2, 96, axis), a3)
-    return y0, y1, y2, y3
+def pick_blocks(lines, block):
+    low = jnp.where(block == 0, lines[0], lines[1])
+    return jnp.where(block < 2, low, jnp.where(block == 2, lines[2], lines[3]))
+
+
+def turned_blocks(lines):
+    block = lane_index(lines[0].shape) // SIDE
+    result = []
+    for k in range(FOUR):
+        y = pick_blocks([lines[(p - k) % FOUR] for p in range(FOUR)], block)
+        result.append(pltpu.roll(y, LANES - SIDE * k, y.ndim - 1) if k else y)
+    return result
 
 
 def spread_blocks(y):
@@ -78,15 +77,12 @@
     )
 
 
-def message_kernel(image_ref, labels_ref, column_ref, row_ref):
-    image = image_ref[...]
+def message_kernel(image_ref, labels_ref, column_ref):
     hot = labels_ref[...].astype(jnp.float32)
     labels = jnp.broadcast_to(jnp.concatenate([hot] * FOUR, axis=1), (8, LANES))
     for d in range(8):
-        column_ref[d, pl.ds(0, 24), :] = image
+        column_ref[d, pl.ds(0, 24), :] = image_ref[...]
         column_ref[d, pl.ds(24, 8), :] = labels
-    for d in range(row_ref.shape[0]):
-        row_ref[d] = image
 
 
 def column_maps(images_ref, pack_ref):
@@ -125,7 +121,7 @@
 
     squares = [0.0] * FOUR
     for c in range(3):
-        planes = swap_blocks(*[images(i, c) for i in range(FOUR)])
+        planes = turned_blocks([images(i, c) for i in range(FOUR)])
         for k in range(FOUR):
             rows_ref[c, k] = FIRST * planes[k]
             squares[k] = squares[k] + planes[k] * planes[k]
@@ -178,16 +174,15 @@
     return value, slope, root * inverse, inside
 
 
-def group_maps(rows_ref, pack_ref, units_ref, bump):
+def forward_maps(rows_ref, pack_ref, state_ref, bump):
     keep_left, keep_right = edge_masks((8, LANES))
 
     def row(c, r):
         return jnp.broadcast_to(rows_ref[c, r % FOUR, pl.ds(r // FOUR, 1), :], (8, LANES))
 
-    cross, value_sum, slope_sum, dsig_sum, ds2_sum, dtheta_sum = {}, {}, {}, {}, {}, {}
-    kept = {}
+    cross, value_sum, slope_sum = {}, {}, {}
     total = jnp.zeros((8, LANES), jnp.float32)
-    for step in range(0, SIDE + 10, 2):
+    for step in range(0, SIDE + 6, 2):
         for r in (step, step + 1):
             if r < SIDE:
                 x = sum(row(c, r) * pack_ref[c, r] for c in range(3))
@@ -198,16 +193,13 @@
                 inverse = row(3, r) * pack_ref[3, r]
                 scale = row(4, r) * pack_ref[4, r]
                 value, slope, weight, inside = arc(sigma, inverse, scale, ALPHA1, None)
+                product = slope * sigma
                 value_sum[r] = across(value, keep_left, keep_right)
-                slope_sum[r] = across(slope * sigma, keep_left, keep_right)
-                if units_ref is not None:
-                    kept[r] = (
-                        sigma,
-                        value,
-                        slope,
-                        jnp.where(inside, slope, 0.0),
-                        jnp.where(inside, sigma * weight, 0.0),
-                    )
+                slope_sum[r] = across(product, keep_left, keep_right)
+                state_ref[r] = sigma
+                state_ref[SIDE + r] = value
+                state_ref[2 * SIDE + r] = jnp.where(inside, slope, -slope)
+                state_ref[3 * SIDE + r] = jnp.where(inside, sigma * weight, 0.0)
         base = step - 4
         if 0 <= base < SIDE:
             for r, sigma, more in zip(
@@ -220,27 +212,35 @@
                 scale = row(6, r) * pack_ref[6, r]
                 value, slope, weight, inside = arc(sigma, inverse, scale, ALPHA2, bump)
                 total = total + (value + slope * theta)
-                if units_ref is not None:
-                    dsigma = jnp.where(inside, slope + theta * weight, 0.0)
-                    units_ref[2, r] = value - dsigma * sigma
-                    ds2_sum[r] = across(slope, keep_left, keep_right)
-                    dsig_sum[r] = across(dsigma + slope, keep_left, keep_right)
-        if units_ref is None:
-            continue
-        base = step - 6
+                dsigma = jnp.where(inside, slope + theta * weight, 0.0)
+                state_ref[4 * SIDE + r] = slope
+                state_ref[5 * SIDE + r] = dsigma + slope
+                state_ref[6 * SIDE + r] = value - dsigma * sigma
+    return total
+
+
+def backward_maps(state_ref, units_ref):
+    keep_left, keep_right = edge_masks((8, LANES))
+    dslope, dsigma, dtheta = {}, {}, {}
+    for step in range(0, SIDE + 6, 2):
+        for r in (step, step + 1):
+            if r < SIDE:
+                dslope[r] = across(state_ref[4 * SIDE + r], keep_left, keep_right)
+                dsigma[r] = across(state_ref[5 * SIDE + r], keep_left, keep_right)
+        base = step - 2
         if 0 <= base < SIDE:
             for r, dvalue, dproduct in zip(
-                (base, base + 1), vertical_pair(dsig_sum, base), vertical_pair(ds2_sum, base)
+                (base, base + 1), vertical_pair(dsigma, base), vertical_pair(dslope, base)
             ):
-                sigma, value, slope, slope_in, weight_in = kept.pop(r)
-                inner = slope_in * dvalue + dproduct * weight_in
-                units_ref[1, r] = value * dvalue - inner * sigma
-                dtheta_sum[r] = across(inner + dproduct * slope, keep_left, keep_right)
-        base = step - 8
+                slope = state_ref[2 * SIDE + r]
+                inner = jnp.maximum(slope, 0.0) * dvalue + dproduct * state_ref[3 * SIDE + r]
+                squeeze = state_ref[SIDE + r] * dvalue - inner * state_ref[r]
+                units_ref[SIDE + r] = squeeze
+                dtheta[r] = across(inner + dproduct * jnp.abs(slope), keep_left, keep_right)
+        base = step - 4
         if 0 <= base < SIDE:
-            for r, unit in zip((base, base + 1), vertical_pair(dtheta_sum, base)):
-                units_ref[0, r] = unit
-    return total
+            for r, unit in zip((base, base + 1), vertical_pair(dtheta, base)):
+                units_ref[r] = unit
 
 
 def sum_entries(totals_ref):
@@ -256,6 +256,12 @@
     totals_ref[:, pl.ds(pl.multiple_of(group * LANES, LANES), LANES)] = total
 
 
+def keep_planes(planes_ref, state_ref, group):
+    for c in range(3):
+        for k in range(FOUR):
+            state_ref[group, MAPS + FOUR * c + k] = planes_ref[group, c, k]
+
+
 def own_bump(group):
     image = group * FOUR + lane_index((8, LANES)) // SIDE
     column = lax.broadcasted_iota(jnp.int32, (8, LANES), 0)
@@ -268,43 +274,58 @@
     return pltpu.make_async_copy(units_ref.at[group], units_hbm.at[group], sems.at[group])
 
 
-def row_kernel(images_ref, planes_ref):
+def row_kernel(images_ref, own_ref, planes_ref, row_ref):
+    place = lax.axis_index("sup") // 2 % FOUR
+    own = pltpu.roll(own_ref[...], SIDE * place, 1)
+    for d in range(row_ref.shape[0]):
+        row_ref[d] = own
     for group in range(8):
 
         def image(i, c, group=group):
             n = group * FOUR + i
             lines = [images_ref[c, pl.ds(n, 1), pl.ds(s * LANES, LANES)] for s in range(8)]
-            return jnp.concatenate(lines, axis=0)
+            x = jnp.concatenate(lines, axis=0)
+            return pltpu.roll(x, SIDE * i, 1) if i else x
 
         row_maps(image, planes_ref.at[group])
 
 
 def target_kernel(
-    planes_ref, columns_ref, entries_ref, pack_ref, inverses_ref, units_hbm, units_ref, totals_ref, sems
+    planes_ref,
+    columns_ref,
+    entries_ref,
+    pack_ref,
+    state_hbm,
+    state_ref,
+    totals_ref,
+    sems,
 ):
     column_maps(columns_ref, pack_ref)
-    block = lane_index((8, LANES)) // SIDE
-    for n in range(2):
-        for s in range(8):
-            inverses_ref[n, s] = pick_blocks([pack_ref[3 + 2 * n, 4 * s + k] for k in range(FOUR)], block)
 
     def body(group, carry):
-        keep_total(
-            totals_ref,
-            group,
-            group_maps(planes_ref.at[group], pack_ref, units_ref.at[group], None),
-        )
-        copy_out(units_ref, units_hbm, sems, group).start()
+        total = forward_maps(planes_ref.at[group], pack_ref, state_ref.at[group], None)
+        keep_total(totals_ref, group, total)
+        keep_planes(planes_ref, state_ref, group)
+        copy_out(state_ref, state_hbm, sems, group).start()
         return carry
 
     lax.fori_loop(0, 8, body, 0)
     entries_ref[...] = sum_entries(totals_ref)
     for group in range(8):
-        copy_out(units_ref, units_hbm, sems, group).wait()
+        copy_out(state_ref, state_hbm, sems, group).wait()
 
 
 def entries_kernel(
-    own_ref, other_ref, pack_ref, entries_t_ref, payload_ref, planes_ref, totals_ref
+    own_ref,
+    other_ref,
+    pack_ref,
+    entries_t_ref,
+    payload_ref,
+    state_hbm,
+    planes_ref,
+    state_ref,
+    totals_ref,
+    sems,
 ):
     for half, images_ref in enumerate((own_ref, other_ref)):
         for group in range(FOUR):
@@ -314,8 +335,12 @@
             )
 
     def body(group, carry):
-        total = group_maps(planes_ref.at[group], pack_ref, None, own_bump(group))
+        total = forward_maps(
+            planes_ref.at[group], pack_ref, state_ref.at[group], own_bump(group)
+        )
         keep_total(totals_ref, group, total)
+        keep_planes(planes_ref, state_ref, group)
+        copy_out(state_ref, state_hbm, sems, group).start()
         return carry
 
     lax.fori_loop(0, 8, body, 0)
@@ -326,19 +351,35 @@
     entries = jnp.where(lax.axis_index("sup") % 2 == 1, turned, entries)
     both = entries + pltpu.roll(entries_t_ref[...], SIDE, 1)
     both = both + pltpu.roll(pltpu.roll(both, 64, 1), FOUR, 0)
+    both = pltpu.roll(both, SIDE * (lax.axis_index("tgt") % FOUR), 1)
     for d in range(payload_ref.shape[0]):
         payload_ref[d] = both[:FOUR]
-
-
-def units_kernel(planes_ref, pack_ref, units_hbm, units_ref, sems):
-    def body(group, carry):
-        group_maps(planes_ref.at[group], pack_ref, units_ref.at[group], own_bump(group))
-        copy_out(units_ref, units_hbm, sems, group).start()
-        return carry
-
-    lax.fori_loop(0, 8, body, 0)
     for group in range(8):
-        copy_out(units_ref, units_hbm, sems, group).wait()
+        copy_out(state_ref, state_hbm, sems, group).wait()
+
+
+def units_kernel(state_t_hbm, state_s_hbm, units_hbm, state_ref, units_ref, in_sems, out_sems):
+    def copy_in(place, source, group):
+        return pltpu.make_async_copy(
+            source.at[group, pl.ds(0, 6 * SIDE)], state_ref.at[place], in_sems.at[place]
+        )
+
+    parts = ((0, state_t_hbm), (8, state_s_hbm))
+    for place, source in parts:
+        for group in range(8):
+            copy_in(place + group, source, group).start()
+
+    for place, source in parts:
+
+        def body(group, carry, place=place, source=source):
+            copy_in(place + group, source, group).wait()
+            backward_maps(state_ref.at[place + group], units_ref.at[place + group])
+            copy_out(units_ref, units_hbm, out_sems, place + group).start()
+            return carry
+
+        lax.fori_loop(0, 8, body, 0)
+    for group in range(16):
+        copy_out(units_ref, units_hbm, out_sems, group).wait()
 
 
 def dot(a, b):
@@ -375,11 +416,6 @@
     high, middle = split(a, 2)
     first = dot(jnp.concatenate([high, middle], axis=0), b[0])
     return first[:16] + (first[16:] + dot(high, b[1]))
-
-
-def pick_blocks(lines, block):
-    low = jnp.where(block == 0, lines[0], lines[1])
-    return jnp.where(block < 2, low, jnp.where(block == 2, lines[2], lines[3]))
 
 
 def merge_blocks(lines, block):
@@ -404,22 +440,20 @@
 
 
 def solve_kernel(
-    own_hbm,
-    other_hbm,
+    own_ref,
+    other_ref,
     support_labels_ref,
-    columns_hbm,
-    inverses_hbm,
-    units_t_hbm,
-    units_s_hbm,
-    planes_t_hbm,
-    planes_s_hbm,
+    columns_ref,
+    pack_hbm,
+    units_hbm,
+    state_t_hbm,
+    state_s_hbm,
+    grad_hbm,
+    objective_ref,
     grad_ref,
-    objective_ref,
-    received_ref,
-    columns_ref,
     inverses_ref,
     units_ref,
-    planes_ref,
+    second_ref,
     kernel_ref,
     inverse_ref,
     matrix_parts,
@@ -434,14 +468,11 @@
         pltpu.make_async_copy(source, target, sems.at[n])
         for n, (source, target) in enumerate(
             [
-                (own_hbm, received_ref.at[core]),
-                (other_hbm, received_ref.at[1 - core]),
-                (columns_hbm, columns_ref),
-                (inverses_hbm, inverses_ref),
-                (units_t_hbm, units_ref.at[pl.ds(0, 8)]),
-                (units_s_hbm, units_ref.at[pl.ds(8, 8)]),
-                (planes_t_hbm.at[:, pl.ds(0, 3)], planes_ref.at[pl.ds(0, 8)]),
-                (planes_s_hbm.at[:, pl.ds(0, 3)], planes_ref.at[pl.ds(8, 8)]),
+                (pack_hbm.at[3], inverses_ref.at[0]),
+                (pack_hbm.at[5], inverses_ref.at[1]),
+                (units_hbm, units_ref),
+                (state_t_hbm.at[:, pl.ds(6 * SIDE, SIDE + 12)], second_ref.at[pl.ds(0, 8)]),
+                (state_s_hbm.at[:, pl.ds(6 * SIDE, SIDE + 12)], second_ref.at[pl.ds(8, 8)]),
             ]
         )
     ]
@@ -449,17 +480,17 @@
         copy.start()
 
     count = 256
-    for copy in copies[:2]:
-        copy.wait()
-    for half in range(2):
+    for half, source_ref in enumerate((own_ref, other_ref)):
+        first = 16 * (core if half == 0 else 1 - core)
         for j in range(FOUR):
             for h in range(2):
                 blocks = []
                 for i in range(FOUR):
                     start = (FOUR * h + i) * 16 * FOUR + j
-                    blocks.append(received_ref[half, pl.ds(start, 16, stride=FOUR), :])
-                for b, y in enumerate(swap_blocks(*blocks)):
-                    rows = pl.ds((FOUR * (b // 2) + j) * 32 + 16 * half, 16)
+                    blocks.append(source_ref[pl.ds(start, 16, stride=FOUR), :])
+                for b, y in enumerate(turned_blocks(blocks)):
+                    start = (FOUR * (b // 2) + j) * 32 + first
+                    rows = pl.ds(pl.multiple_of(start, 16), 16)
                     lanes = pl.ds(h * LANES, LANES)
                     if b % 2 == 0:
                         kernel_ref[rows, lanes] = y
@@ -474,14 +505,37 @@
     trace = jnp.sum(jnp.where(eye, matrix, 0.0))
     ridge = 0.1 * trace / count
     matrix = matrix + jnp.where(eye, ridge, 0.0)
-    bound = jnp.max(jnp.sum(jnp.abs(matrix), axis=0, keepdims=True))
-    spread = (bound - ridge) / (bound + ridge)
-    start = 2.0 / (bound + ridge)
+    for n, part in enumerate(split(matrix, 3)):
+        matrix_parts[n] = part
+
+    def whole(x):
+        return jnp.sum(x, axis=1, keepdims=True)
+
+    v_row, v_col = jnp.sum(matrix, axis=0, keepdims=True), whole(matrix)
+    norm = lax.rsqrt(whole(v_row * v_row))
+    v_row, v_col = v_row * norm, v_col * norm
+    w_row, w_col = jnp.sum(matrix * v_col, axis=0, keepdims=True), whole(matrix * v_row)
+    top = whole(w_row * v_row)
+    off = w_row - top * v_row
+    rest = jnp.sum(jnp.abs(matrix - (top * v_col) * v_row), axis=0, keepdims=True)
+    rest = jnp.max(rest, axis=1, keepdims=True)
+    alpha = 2.0 / (rest + ridge)
+    limit = jnp.maximum(alpha * rest, 1.0) + jnp.sqrt(alpha / top * whole(off * off))
+    floor = alpha * ridge
+    scale = 2.0 / (limit + floor)
+    spread = (limit - floor) / (limit + floor)
     square = spread * spread
     gain = 2.0 / (2.0 - square)
-    inverse_ref[...] = (gain * start) * (jnp.where(eye, 2.0, 0.0) - start * matrix)
-    for n, part in enumerate(split(matrix, 3)):
-        matrix_parts[n] = part
+    gamma = scale * (1.0 / top - alpha)
+    alpha = scale * alpha
+    side = gain * ((2.0 * gamma - gamma * gamma * top) * v_col - (alpha * gamma) * w_col)
+    inverse_ref[...] = (
+        jnp.where(eye, 2.0 * gain * alpha, 0.0)
+        - (gain * alpha * alpha) * matrix
+        + side * v_row
+        - (gain * alpha * gamma * v_col) * w_row
+    )
+    square = square[0, 0]
 
     def improve(delta):
         square = delta * delta
@@ -492,22 +546,9 @@
         inverse_ref[...] = gain * (x + product3(parts, split(error, 2)))
         return square / (2.0 - square)
 
-    lax.while_loop(lambda delta: delta > 3e-3, improve, square / (2.0 - square))
+    lax.while_loop(lambda delta: delta > 1e-3, improve, square / (2.0 - square))
     for n, part in enumerate(split(inverse_ref[...], 2)):
         inverse_parts[n] = part
-
-    def solve(right):
-        def refine(state):
-            guess, _, rounds = state
-            rest = right - thin_exact(guess, matrix_parts)
-            step = thin_near(rest, inverse_parts)
-            guess = guess + step
-            return guess, jnp.sum(step * step) / jnp.sum(guess * guess), rounds + 1
-
-        def going(state):
-            return jnp.logical_and(state[1] > 1e-9, state[2] < 40)
-
-        return lax.while_loop(going, refine, (thin_near(right, inverse_parts), 1.0, 0))[0]
 
     class_id = lax.broadcasted_iota(jnp.int32, (16, count), 0)
 
@@ -515,9 +556,7 @@
         hot = (class_id == labels).astype(jnp.float32) - 0.1
         return jnp.where(class_id < CLASSES, hot, 0.0)
 
-    coeffs = solve(one_hot(support_labels_ref[...]))
-    for copy in copies[2:4]:
-        copy.wait()
+    support_hot = one_hot(support_labels_ref[...])
     lane1 = lane_index((1, LANES))
     halves = []
     for h in range(2):
@@ -525,9 +564,38 @@
         line = [jnp.where(lane1 // SIDE == i, x, 0.0) for i, x in enumerate(line)]
         halves.append((line[0] + line[1]) + (line[2] + line[3]))
     target_labels = jnp.concatenate(halves, axis=1).astype(jnp.int32)
-    residual = thin_exact(coeffs, cross_parts) - one_hot(target_labels)
+    target_hot = one_hot(target_labels)
+
+    def refine(coeffs, adjoint):
+        step = thin_near(support_hot - thin_exact(coeffs, matrix_parts), inverse_parts)
+        coeffs = coeffs + step
+        residual = thin_exact(coeffs, cross_parts) - target_hot
+        right = thin_exact(residual, cross_parts, dot_nt)
+        if adjoint is None:
+            adjoint = thin_near(right, inverse_parts)
+        more = thin_near(right - thin_exact(adjoint, matrix_parts), inverse_parts)
+        adjoint = adjoint + more
+        moved = jnp.maximum(
+            whole(jnp.sum(step * step, axis=0, keepdims=True))
+            / whole(jnp.sum(coeffs * coeffs, axis=0, keepdims=True)),
+            whole(jnp.sum(more * more, axis=0, keepdims=True))
+            / whole(jnp.sum(adjoint * adjoint, axis=0, keepdims=True)),
+        )
+        return coeffs, adjoint, residual, moved
+
+    coeffs, adjoint, residual, moved = refine(thin_near(support_hot, inverse_parts), None)
+
+    def again(state):
+        coeffs, adjoint, _, moved, _, rounds = state
+        coeffs, adjoint, residual, now = refine(coeffs, adjoint)
+        return coeffs, adjoint, residual, now, (now * now / moved)[0, 0], rounds + 1
+
+    coeffs, adjoint, residual, _, _, _ = lax.while_loop(
+        lambda state: jnp.logical_and(state[4] > 1e-13, state[5] < 40),
+        again,
+        (coeffs, adjoint, residual, moved, (moved * moved)[0, 0], 0),
+    )
     objective_ref[...] = jnp.full((8, LANES), 0.5 * jnp.sum(residual * residual), jnp.float32)
-    adjoint = solve(thin_exact(residual, cross_parts, dot_nt))
     trace_grad = -jnp.sum(adjoint * coeffs)
 
     mine_t = lax.axis_index("tgt")
@@ -564,7 +632,7 @@
         weights_ref[g] = wide[:8, g * LANES : (g + 1) * LANES]
         weights_ref[8 + lax.rem(g + FOUR * core, 8)] = wide[8:, g * LANES : (g + 1) * LANES]
 
-    for copy in copies[4:]:
+    for copy in copies:
         copy.wait()
 
     block = lane8 // SIDE
@@ -576,13 +644,16 @@
             sums = [None] * 5
             for g in range(16):
                 weight = weights_ref[g]
-                dx = weight * units_ref[g, 0, r]
+                dx = weight * units_ref[g, r]
                 terms = [
-                    dx * jnp.broadcast_to(planes_ref[g, c, k, pl.ds(s, 1), :], (8, LANES))
+                    dx
+                    * jnp.broadcast_to(
+                        second_ref[g, SIDE + FOUR * c + k, pl.ds(s, 1), :], (8, LANES)
+                    )
                     for c in range(3)
                 ]
-                terms.append(weight * units_ref[g, 1, r])
-                terms.append(weight * units_ref[g, 2, r])
+                terms.append(weight * units_ref[g, SIDE + r])
+                terms.append(weight * second_ref[g, r])
                 sums = [t if a is None else a + t for a, t in zip(sums, terms)]
             for n in range(5):
                 lines[n].append(sums[n])
@@ -590,14 +661,18 @@
             grads_ref[n, s] = merge_blocks(lines[n], block)
         return carry
 
-    lax.fori_loop(0, 8, gather_line, 0, unroll=2)
+    lax.fori_loop(0, 8, gather_line, 0, unroll=4)
 
     masks = edge_masks((8, LANES))
-    second = [0.5 * inverses_ref[1, s] * inverses_ref[1, s] * grads_ref[4, s] for s in range(8)]
+
+    def half_over_variance(n, s):
+        inverse = pick_blocks([inverses_ref[n, FOUR * s + k] for k in range(FOUR)], block)
+        return 0.5 * inverse * inverse
+
+    second = [half_over_variance(1, s) * grads_ref[4, s] for s in range(8)]
     second = image_stencil(second, masks, block)
     first = [
-        0.5 * inverses_ref[0, s] * inverses_ref[0, s] * grads_ref[3, s] + (0.5 * SECOND) * second[s]
-        for s in range(8)
+        half_over_variance(0, s) * grads_ref[3, s] + (0.5 * SECOND) * second[s] for s in range(8)
     ]
     first = image_stencil(first, masks, block)
     for s in range(8):
@@ -606,30 +681,34 @@
             grad_ref[pl.ds(c * 8 + s, 8, stride=24), :] = (
                 grads_ref[c, s] + (2.0 * FIRST) * first[s] * image
             )
+    copy = pltpu.make_async_copy(grad_ref, grad_hbm, sems.at[5])
+    copy.start()
+    copy.wait()
 
 
 def f32(*shape):
     return jax.ShapeDtypeStruct(shape, jnp.float32)
 
 
-HBM = pl.BlockSpec(memory_space=pl.ANY)
+HBM = pl.BlockSpec(memory_space=pltpu.HBM)
 VMEM = pl.BlockSpec(memory_space=pltpu.VMEM)
 
 
-def call(kernel, ins, outs, shapes, scratch, work=0):
+def call(kernel, ins, outs, shapes, scratch, limit, work=0):
     return pl.pallas_call(
         kernel,
         in_specs=ins,
         out_specs=outs,
         out_shape=shapes,
         scratch_shapes=scratch,
-        compiler_params=pltpu.CompilerParams(vmem_limit_bytes=VMEM_LIMIT),
+        compiler_params=pltpu.CompilerParams(vmem_limit_bytes=limit * KIB),
         cost_estimate=pl.CostEstimate(flops=work, bytes_accessed=4 << 20, transcendentals=0),
     )
 
 
 PLANES = (8, 7, FOUR, 8, LANES)
-UNITS = (8, 3, SIDE, 8, LANES)
+STATE = (8, MAPS + 12, 8, LANES)
+UNITS = (16, 2 * SIDE, 8, LANES)
 PACK = (7, SIDE, 8, LANES)
 WORK = 256 * 1024 * 140
 
@@ -640,62 +719,75 @@
     chips = [[2 * chip + core for chip in range(128)] for core in range(2)]
     cores = [(device, device ^ 1) for device in range(32)]
 
-    column_message, row_message = call(
-        message_kernel, [VMEM] * 2, [VMEM] * 2, [f32(8, 32, LANES), f32(16, 24, LANES)], []
-    )(support.reshape(24, LANES), target_labels.reshape(1, 32))
+    image = support.reshape(24, LANES)
+    column_message = call(
+        message_kernel, [VMEM] * 2, VMEM, f32(8, 32, LANES), [], 60 * KIB
+    )(image, target_labels.reshape(1, 32))
     columns = lax.all_to_all(column_message, "tgt", 0, 0, tiled=True).reshape(256, LANES)
-    planes_t = call(row_kernel, [VMEM], VMEM, f32(*PLANES), [], WORK // 2)(
-        targets.transpose(1, 0, 2)
-    )
+    planes_t, row_message = call(
+        row_kernel, [VMEM] * 2, [VMEM] * 2, [f32(*PLANES), f32(16, 24, LANES)], [], 48 * KIB, WORK // 2
+    )(targets.transpose(1, 0, 2), image)
     labels = support_labels.reshape(8, 16, 2).transpose(0, 2, 1).reshape(1, 256)
     columns, planes_t, row_message, labels = lax.optimization_barrier(
         (columns, planes_t, row_message, labels)
     )
     rows = lax.all_to_all(row_message, "sup", 0, 0, tiled=True, axis_index_groups=zx)
-    entries_t, pack, inverses, units_t = call(
+    entries_t, pack, state_t = call(
         target_kernel,
         [VMEM] * 2,
-        [VMEM] * 3 + [HBM],
-        [f32(8, LANES), f32(*PACK), f32(2, 8, 8, LANES), f32(*UNITS)],
+        [VMEM] * 2 + [HBM],
+        [f32(8, LANES), f32(*PACK), f32(*STATE)],
         [
-            scratch(UNITS, jnp.float32),
+            scratch(STATE, jnp.float32),
             scratch((8, 1024), jnp.float32),
             pltpu.SemaphoreType.DMA((8,)),
         ],
+        51500,
         WORK,
     )(planes_t, columns)
     rows, entries_t = lax.optimization_barrier((rows, entries_t))
     rows_other = lax.ppermute(rows, "sup", cores)
-    payload, planes_s = call(
+    payload, state_s = call(
         entries_kernel,
         [VMEM] * 4,
-        [VMEM] * 2,
-        [f32(128, FOUR, LANES), f32(*PLANES)],
-        [scratch((8, 1024), jnp.float32)],
+        [VMEM, HBM],
+        [f32(128, FOUR, LANES), f32(*STATE)],
+        [
+            scratch(PLANES, jnp.float32),
+            scratch(STATE, jnp.float32),
+            scratch((8, 1024), jnp.float32),
+            pltpu.SemaphoreType.DMA((8,)),
+        ],
+        52500,
         WORK // 2,
     )(rows, rows_other, pack, entries_t)
     received = lax.all_to_all(payload, BOTH, 0, 0, tiled=True, axis_index_groups=chips)
-    units_s = call(
+    units = call(
         units_kernel,
-        [VMEM] * 2,
+        [HBM] * 2,
         HBM,
         f32(*UNITS),
-        [scratch(UNITS, jnp.float32), pltpu.SemaphoreType.DMA((8,))],
+        [
+            scratch((16, 6 * SIDE, 8, LANES), jnp.float32),
+            scratch(UNITS, jnp.float32),
+            pltpu.SemaphoreType.DMA((16,)),
+            pltpu.SemaphoreType.DMA((16,)),
+        ],
+        54200,
         WORK,
-    )(planes_s, pack)
-    received, units_s = lax.optimization_barrier((received, units_s))
+    )(state_t, state_s)
+    received, units = lax.optimization_barrier((received, units))
     received_other = lax.ppermute(received, "sup", cores)
     partial, objective = call(
         solve_kernel,
-        [HBM] * 2 + [VMEM] + [HBM] * 6,
-        [VMEM] * 2,
+        [VMEM] * 4 + [HBM] * 4,
+        [HBM, VMEM],
         [f32(192, LANES), f32(8, LANES)],
         [
-            scratch((2, 512, LANES), jnp.float32),
-            scratch((256, LANES), jnp.float32),
-            scratch((2, 8, 8, LANES), jnp.float32),
-            scratch((16, 3, SIDE, 8, LANES), jnp.float32),
-            scratch((16, 3, FOUR, 8, LANES), jnp.float32),
+            scratch((192, LANES), jnp.float32),
+            scratch((2, SIDE, 8, LANES), jnp.float32),
+            scratch((16, 2 * SIDE, 8, LANES), jnp.float32),
+            scratch((16, SIDE + 12, 8, LANES), jnp.float32),
             scratch((256, 256), jnp.float32),
             scratch((256, 256), jnp.float32),
             scratch((3, 256, 256), jnp.bfloat16),
@@ -703,19 +795,19 @@
             scratch((2, 256, 256), jnp.bfloat16),
             scratch((16, 8, LANES), jnp.float32),
             scratch((5, 8, 8, LANES), jnp.float32),
-            pltpu.SemaphoreType.DMA((8,)),
+            pltpu.SemaphoreType.DMA((6,)),
         ],
+        54200,
         WORK,
     )(
         received.reshape(512, LANES),
         received_other.reshape(512, LANES),
         labels,
         columns,
-        inverses,
-        units_t,
-        units_s,
-        planes_t,
-        planes_s,
+        pack,
+        units,
+        state_t,
+        state_s,
     )
     pieces = lax.all_to_all(partial.reshape(8, 24, LANES), "tgt", 0, 0, tiled=True)
     return jnp.sum(pieces, axis=0).reshape(1, 3, 1024), objective[0, 0]

time: 99.4 us -> 88.5 us (0.89)
  Pallas kernels: 43.5 us -> 34 us
  starting transfers between devices: 35.1 us -> 31.6 us
  waiting for transfers between devices: 14.6 us -> 17.7 us
    pallas_call x6, Pallas kernels: 43.5 us -> 34 us  [the longest x1 10.4 us: on_device(): call(units_kernel, [HBM] * 2, HBM, f32(*UNITS), [scratch((16, 6 * SIDE, 8...]
    all_to_all x1, starting transfers between devices: 11.2 us -> 6.43 us  [on_device(): lax.all_to_all(payload, BOTH, 0, 0, tiled=True, axis_index_groups=chips)]
    all_to_all x1, waiting for transfers between devices: 0.01 us -> 3.28 us  [on_device(): lax.all_to_all(row_message, 'sup', 0, 0, tiled=True, axis_index_groups=zx)]
    all_to_all x1, waiting for transfers between devices: 4.06 us -> 2.72 us  [on_device(): lax.all_to_all(payload, BOTH, 0, 0, tiled=True, axis_index_groups=chips)]
    ppermute x1, starting transfers between devices: 2.47 us -> 3.53 us  [on_device(): rows_other = lax.ppermute(rows, 'sup', cores)]
  transfers between devices with their start and end apart: 6 -> 6, of which waited for: 5 -> 6; matrix products, arithmetic and copies ran while one was open for 3% -> 2% of each run, Pallas kernels for 23% -> 20%
where the time goes in v3:
time: 88.5 us; the launch traced here: 87.8 us
  Pallas kernels  34 us (38%)
  starting transfers between devices  31.6 us (36%)
  waiting for transfers between devices  17.7 us (20%)
  local copies, waits for them, and re-layouts  3.25 us (4%)
    pallas_call x1, Pallas kernels, on_device(): call(units_kernel, [HBM] * 2, HBM, f32(*UNITS), [scratch((16, 6 * SIDE, 8...  10.4 us
    pallas_call x1, Pallas kernels, on_device(): call(solve_kernel, [VMEM] * 4 + [HBM] * 4, [HBM, VMEM], [f32(192, LANES),...  8.79 us
    all_to_all x1, starting transfers between devices, on_device(): lax.all_to_all(row_message, 'sup', 0, 0, tiled=True, axis_index_groups=zx)  8.32 us
    all_to_all x1, starting transfers between devices, on_device(): lax.all_to_all(column_message, 'tgt', 0, 0, tiled=True).reshape(256, LANES)  7.48 us
    pallas_call x1, Pallas kernels, on_device(): call(entries_kernel, [VMEM] * 4, [VMEM, HBM], [f32(128, FOUR, LANES), f32...  6.45 us
    all_to_all x1, starting transfers between devices, on_device(): lax.all_to_all(payload, BOTH, 0, 0, tiled=True, axis_index_groups=chips)  6.43 us
    all_to_all x1, waiting for transfers between devices, on_device(): lax.all_to_all(partial.reshape(8, 24, LANES), 'tgt', 0, 0, tiled=True)  6.31 us
    pallas_call x1, Pallas kernels, on_device(): call(target_kernel, [VMEM] * 2, [VMEM] * 2 + [HBM], [f32(8, LANES), f32(*...  5.74 us
  transfers between devices with their start and end apart: 6, of which 6 were waited for; matrix products, arithmetic and copies ran while one was open for 2% of the time, Pallas kernels for 20%

profile of v3, /device:TPU:1, one launch (start us, length us, event | category | flops | bytes accessed | tf_op | source)
XLA Modules:
  0.0 87.8 jit_solution(8044787884382012928)
XLA Ops:
  0.6 1.4 %shard_map.59 = f32[8,32,128]{2,1,0:T(8,128)} custom-call(f32[24,128]{1,0:T(8,128)} %bitcast.15, s32[1,32]{1,0:T(1,128)} %bitcast.19), custom_call_target="tpu_custom_call" | custom-call | bytes 4194304 | tf_op jit(solution)/shard_map/pallas_call | solution.py:723
  2.1 7.5 %all-to-all-start = ((f32[8,32,128]{2,1,0:T(8,128)}), f32[8,32,128]{2,1,0:T(8,128)S(1)}, u32[]{:S(2)}, u32[]{:S(2)}) async-start(f32[8,32,128]{2,1,0:T(8,128)} %shard_map.59), calls=%async_computation | async-start | bytes 262144 | tf_op jit(solution)/shard_map/all_to_all | solution.py:726
  9.5 0.8 reshape.34
  10.4 0.1 copy.6
  10.6 1.0 %copy-done.1 = f32[32,3,1024]{2,0,1:T(8,128)S(1)} copy-done((f32[32,3,1024]{2,0,1:T(8,128)S(1)}, f32[32,3,1024]{2,0,1:T(8,128)}, u32[]{:S(2)}) %copy-start.1) | copy-done | bytes 393240
  11.6 0.7 copy-done.2
  12.3 1.2 %shard_map.60 = (f32[8,7,4,8,128]{4,3,2,1,0:T(8,128)S(1)}, f32[16,24,128]{2,1,0:T(8,128)}) custom-call(f32[3,32,1024]{2,1,0:T(8,128)S(1)} %bitcast.13, f32[24,128]{1,0:T(8,128)S(1)} %bitcast.16), custom_call_target="tpu_custom_call" | custom-call | flops 18350080 | bytes 4194304 | tf_op jit(solution)/shard_map/pallas_call | solution.py:727
  13.5 3.1 %all-to-all-done = f32[8,32,128]{2,1,0:T(8,128)S(1)} async-done(((f32[8,32,128]{2,1,0:T(8,128)}), f32[8,32,128]{2,1,0:T(8,128)S(1)}, u32[]{:S(2)}, u32[]{:S(2)}) %all-to-all-start) | async-done | bytes 131104 | tf_op jit(solution)/shard_map/all_to_all | solution.py:726
  16.6 8.3 %all-to-all-start.1 = ((f32[16,24,128]{2,1,0:T(8,128)}), f32[16,24,128]{2,1,0:T(8,128)S(1)}, u32[]{:S(2)}, u32[]{:S(2)}) async-start(f32[16,24,128]{2,1,0:T(8,128)} %get-tuple-element.21), calls=%async_computation.1 | async-start | bytes 393216 | tf_op jit(solution)/shard_map/all_to_all | solution.py:734
  24.9 5.7 %shard_map.61 = (f32[8,128]{1,0:T(8,128)S(1)}, f32[7,32,8,128]{3,2,1,0:T(8,128)S(1)}, f32[8,236,8,128]{3,2,1,0:T(8,128)}) custom-call(f32[8,7,4,8,128]{4,3,2,1,0:T(8,128)S(1)} %get-tuple-element.22.planes_ref, f32[256,128]{1,0:T(8,128)S(1)} %bitcast.10), custom_call_target="tpu_custom_call" | custom-call | flops 36700160 | bytes 4194304 | tf_op jit(solution)/shard_map/pallas_call | solution.py:735
  30.7 3.3 %all-to-all-done.1.own_ref = f32[16,24,128]{2,1,0:T(8,128)S(1)} async-done(((f32[16,24,128]{2,1,0:T(8,128)}), f32[16,24,128]{2,1,0:T(8,128)S(1)}, u32[]{:S(2)}, u32[]{:S(2)}) %all-to-all-start.1) | async-done | bytes 196640 | tf_op jit(solution)/shard_map/all_to_all | solution.py:734
  34.0 3.5 %collective-permute-start = (f32[16,24,128]{2,1,0:T(8,128)S(1)}, f32[16,24,128]{2,1,0:T(8,128)S(1)}, u32[]{:S(2)}, u32[]{:S(2)}) collective-permute-start(f32[16,24,128]{2,1,0:T(8,128)S(1)} %all-to-all-done.1.own_ref), channel_id=1, source_target_pairs={{0,1},{1,0},{2,3},{3,2},{4,5},{5,4},{6,7},{7,6},{8,9},{9,8},{10,11... | collective-permute-start | bytes 589832 | tf_op jit(solution)/shard_map/ppermute | solution.py:749
  37.5 1.1 %collective-permute-done.other_ref = f32[16,24,128]{2,1,0:T(8,128)S(1)} collective-permute-done((f32[16,24,128]{2,1,0:T(8,128)S(1)}, f32[16,24,128]{2,1,0:T(8,128)S(1)}, u32[]{:S(2)}, u32[]{:S(2)}) %collective-permute-start) | collective-permute-done | bytes 196640 | tf_op jit(solution)/shard_map/ppermute | solution.py:749
  38.6 6.5 %shard_map.62 = (f32[128,4,128]{2,1,0:T(4,128)}, f32[8,236,8,128]{3,2,1,0:T(8,128)}) custom-call(f32[16,24,128]{2,1,0:T(8,128)S(1)} %all-to-all-done.1.own_ref, f32[16,24,128]{2,1,0:T(8,128)S(1)} %collective-permute-done.other_ref, f32[7,32,8,128]{3,2,1,0:T(8,128)S(1)} %get-tuple-element.26.pack_ref.pack_hbm, f32[8,128]{1,0:T(8,128)S(1)} %get-tuple-element.27.entries_t_ref), custom_call_target="tpu_custom_call" | custom-call | flops 18350080 | bytes 4194304 | tf_op jit(solution)/shard_map/pallas_call | solution.py:750
  45.0 6.4 %all-to-all-start.2 = ((f32[128,4,128]{2,1,0:T(4,128)}), f32[128,4,128]{2,1,0:T(4,128)S(1)}, u32[]{:S(2)}, u32[]{:S(2)}) async-start(f32[128,4,128]{2,1,0:T(4,128)} %get-tuple-element.28), calls=%async_computation.2 | async-start | bytes 524288 | tf_op jit(solution)/shard_map/all_to_all | solution.py:764
  51.5 10.4 %shard_map.63.units_hbm = f32[16,64,8,128]{3,2,1,0:T(8,128)} custom-call(f32[8,236,8,128]{3,2,1,0:T(8,128)} %get-tuple-element.29.state_t_hbm, f32[8,236,8,128]{3,2,1,0:T(8,128)} %get-tuple-element.30.state_s_hbm), custom_call_target="tpu_custom_call" | custom-call | flops 36700160 | bytes 4194304 | tf_op jit(solution)/shard_map/pallas_call | solution.py:765
  61.9 2.7 %all-to-all-done.2 = f32[128,4,128]{2,1,0:T(4,128)S(1)} async-done(((f32[128,4,128]{2,1,0:T(4,128)}), f32[128,4,128]{2,1,0:T(4,128)S(1)}, u32[]{:S(2)}, u32[]{:S(2)}) %all-to-all-start.2) | async-done | bytes 262176 | tf_op jit(solution)/shard_map/all_to_all | solution.py:764
  64.6 2.4 %collective-permute-start.1 = (f32[128,4,128]{2,1,0:T(4,128)S(1)}, f32[128,4,128]{2,1,0:T(4,128)S(1)}, u32[]{:S(2)}, u32[]{:S(2)}) collective-permute-start(f32[128,4,128]{2,1,0:T(4,128)S(1)} %all-to-all-done.2), channel_id=1, source_target_pairs={{0,1},{1,0},{2,3},{3,2},{4,5},{5,4},{6,7},{7,6},{8,9},{9,8},{10,11... | collective-permute-start | bytes 786440 | tf_op jit(solution)/shard_map/ppermute | solution.py:780
  67.0 1.2 %collective-permute-done.1 = f32[128,4,128]{2,1,0:T(4,128)S(1)} collective-permute-done((f32[128,4,128]{2,1,0:T(4,128)S(1)}, f32[128,4,128]{2,1,0:T(4,128)S(1)}, u32[]{:S(2)}, u32[]{:S(2)}) %collective-permute-start.1) | collective-permute-done | bytes 262176 | tf_op jit(solution)/shard_map/ppermute | solution.py:780
  68.2 8.8 %shard_map.64 = (f32[192,128]{1,0:T(8,128)}, f32[8,128]{1,0:T(8,128)S(1)}) custom-call(f32[512,128]{1,0:T(8,128)S(1)} %bitcast.12, f32[512,128]{1,0:T(8,128)S(1)} %bitcast.14, s32[1,256]{1,0:T(1,128)S(1)} %reshape.35.support_labels_ref, f32[256,128]{1,0:T(8,128)S(1)} %bitcast.11, f32[7,32,8,128]{3,2,1,0:T(8,128)} %copy-done, ...), custom_call_target="tpu_custom_call" | custom-call | flops 36700160 | bytes 4194304 | tf_op jit(solution)/shard_map/pallas_call | solution.py:781
  77.0 3.4 %all-to-all-start.3 = ((f32[8,24,128]{2,1,0:T(8,128)}), f32[8,24,128]{2,1,0:T(8,128)S(1)}, u32[]{:S(2)}, u32[]{:S(2)}) async-start(f32[8,24,128]{2,1,0:T(8,128)} %bitcast.7), calls=%async_computation.3 | async-start | bytes 196608 | tf_op jit(solution)/shard_map/all_to_all | solution.py:812
  80.4 0.5 slice.3
  80.9 6.3 %all-to-all-done.3 = f32[8,24,128]{2,1,0:T(8,128)S(1)} async-done(((f32[8,24,128]{2,1,0:T(8,128)}), f32[8,24,128]{2,1,0:T(8,128)S(1)}, u32[]{:S(2)}, u32[]{:S(2)}) %all-to-all-start.3) | async-done | bytes 98336 | tf_op jit(solution)/shard_map/all_to_all | solution.py:812
  87.2 0.6 reduce_sum.9
  (5 shorter events, 0.1 us)
Async XLA Ops:
  2.1 14.5 %all-to-all-start = ((f32[8,32,128]{2,1,0:T(8,128)}), f32[8,32,128]{2,1,0:T(8,128)S(1)}, u32[]{:S(2)}, u32[]{:S(2)}) async-start(f32[8,32,128]{2,1,0:T(8,128)} %shard_map.59), calls=%async_computation | async-start | bytes 262144 | tf_op jit(solution)/shard_map/all_to_all | solution.py:726
  10.6 1.0 %copy-start.1 = (f32[32,3,1024]{2,0,1:T(8,128)S(1)}, f32[32,3,1024]{2,0,1:T(8,128)}, u32[]{:S(2)}) copy-start(f32[32,3,1024]{2,0,1:T(8,128)} %param.6) | copy-start | bytes 1179652
  11.6 0.7 copy-start.2
  16.6 17.4 %all-to-all-start.1 = ((f32[16,24,128]{2,1,0:T(8,128)}), f32[16,24,128]{2,1,0:T(8,128)S(1)}, u32[]{:S(2)}, u32[]{:S(2)}) async-start(f32[16,24,128]{2,1,0:T(8,128)} %get-tuple-element.21), calls=%async_computation.1 | async-start | bytes 393216 | tf_op jit(solution)/shard_map/all_to_all | solution.py:734
  30.7 31.2 %copy-start = (f32[7,32,8,128]{3,2,1,0:T(8,128)}, f32[7,32,8,128]{3,2,1,0:T(8,128)S(1)}, u32[]{:S(2)}) copy-start(f32[7,32,8,128]{3,2,1,0:T(8,128)S(1)} %get-tuple-element.26.pack_ref.pack_hbm) | copy-start | bytes 2752516
  34.0 4.6 %collective-permute-start = (f32[16,24,128]{2,1,0:T(8,128)S(1)}, f32[16,24,128]{2,1,0:T(8,128)S(1)}, u32[]{:S(2)}, u32[]{:S(2)}) collective-permute-start(f32[16,24,128]{2,1,0:T(8,128)S(1)} %all-to-all-done.1.own_ref), channel_id=1, source_target_pairs={{0,1},{1,0},{2,3},{3,2},{4,5},{5,4},{6,7},{7,6},{8,9},{9,8},{10,11... | collective-permute-start | bytes 589832 | tf_op jit(solution)/shard_map/ppermute | solution.py:749
  45.0 19.6 %all-to-all-start.2 = ((f32[128,4,128]{2,1,0:T(4,128)}), f32[128,4,128]{2,1,0:T(4,128)S(1)}, u32[]{:S(2)}, u32[]{:S(2)}) async-start(f32[128,4,128]{2,1,0:T(4,128)} %get-tuple-element.28), calls=%async_computation.2 | async-start | bytes 524288 | tf_op jit(solution)/shard_map/all_to_all | solution.py:764
  64.6 3.6 %collective-permute-start.1 = (f32[128,4,128]{2,1,0:T(4,128)S(1)}, f32[128,4,128]{2,1,0:T(4,128)S(1)}, u32[]{:S(2)}, u32[]{:S(2)}) collective-permute-start(f32[128,4,128]{2,1,0:T(4,128)S(1)} %all-to-all-done.2), channel_id=1, source_target_pairs={{0,1},{1,0},{2,3},{3,2},{4,5},{5,4},{6,7},{7,6},{8,9},{9,8},{10,11... | collective-permute-start | bytes 786440 | tf_op jit(solution)/shard_map/ppermute | solution.py:780
  77.0 10.2 %all-to-all-start.3 = ((f32[8,24,128]{2,1,0:T(8,128)}), f32[8,24,128]{2,1,0:T(8,128)S(1)}, u32[]{:S(2)}, u32[]{:S(2)}) async-start(f32[8,24,128]{2,1,0:T(8,128)} %bitcast.7), calls=%async_computation.3 | async-start | bytes 196608 | tf_op jit(solution)/shard_map/all_to_all | solution.py:812

commit v4 on v3

--- a/solution.py
+++ b/solution.py
@@ -77,12 +77,16 @@
     )
 
 
-def message_kernel(image_ref, labels_ref, column_ref):
+def message_kernel(image_ref, labels_ref, column_ref, row_ref):
     hot = labels_ref[...].astype(jnp.float32)
     labels = jnp.broadcast_to(jnp.concatenate([hot] * FOUR, axis=1), (8, LANES))
-    for d in range(8):
-        column_ref[d, pl.ds(0, 24), :] = image_ref[...]
+    image = image_ref[...]
+    for d in range(column_ref.shape[0]):
+        column_ref[d, pl.ds(0, 24), :] = image
         column_ref[d, pl.ds(24, 8), :] = labels
+    turned = pltpu.roll(image, SIDE * (lax.axis_index("sup") // 2 % FOUR), 1)
+    for d in range(row_ref.shape[0]):
+        row_ref[d] = turned
 
 
 def column_maps(images_ref, pack_ref):
@@ -185,7 +189,8 @@
     for step in range(0, SIDE + 6, 2):
         for r in (step, step + 1):
             if r < SIDE:
-                x = sum(row(c, r) * pack_ref[c, r] for c in range(3))
+                x = row(0, r) * pack_ref[0, r] + row(1, r) * pack_ref[1, r]
+                x = x + row(2, r) * pack_ref[2, r]
                 cross[r] = across(x, keep_left, keep_right)
         base = step - 2
         if 0 <= base < SIDE:
@@ -256,10 +261,10 @@
     totals_ref[:, pl.ds(pl.multiple_of(group * LANES, LANES), LANES)] = total
 
 
-def keep_planes(planes_ref, state_ref, group):
+def keep_planes(planes_ref, group, state_ref, place):
     for c in range(3):
         for k in range(FOUR):
-            state_ref[group, MAPS + FOUR * c + k] = planes_ref[group, c, k]
+            state_ref[place, MAPS + FOUR * c + k] = planes_ref[group, c, k]
 
 
 def own_bump(group):
@@ -274,11 +279,7 @@
     return pltpu.make_async_copy(units_ref.at[group], units_hbm.at[group], sems.at[group])
 
 
-def row_kernel(images_ref, own_ref, planes_ref, row_ref):
-    place = lax.axis_index("sup") // 2 % FOUR
-    own = pltpu.roll(own_ref[...], SIDE * place, 1)
-    for d in range(row_ref.shape[0]):
-        row_ref[d] = own
+def row_kernel(images_ref, planes_ref):
     for group in range(8):
 
         def image(i, c, group=group):
@@ -305,7 +306,7 @@
     def body(group, carry):
         total = forward_maps(planes_ref.at[group], pack_ref, state_ref.at[group], None)
         keep_total(totals_ref, group, total)
-        keep_planes(planes_ref, state_ref, group)
+        keep_planes(planes_ref, group, state_ref, group)
         copy_out(state_ref, state_hbm, sems, group).start()
         return carry
 
@@ -315,35 +316,47 @@
         copy_out(state_ref, state_hbm, sems, group).wait()
 
 
+def half_kernel(images_ref, planes_ref):
+    for group in range(FOUR):
+        row_maps(
+            lambda i, c: images_ref[group * FOUR + i, pl.ds(c * 8, 8), :], planes_ref.at[group]
+        )
+
+
 def entries_kernel(
-    own_ref,
+    planes_own_ref,
     other_ref,
     pack_ref,
     entries_t_ref,
-    payload_ref,
+    payload_hbm,
     state_hbm,
     planes_ref,
     state_ref,
     totals_ref,
+    payload_ref,
     sems,
 ):
-    for half, images_ref in enumerate((own_ref, other_ref)):
-        for group in range(FOUR):
-            row_maps(
-                lambda i, c: images_ref[group * FOUR + i, pl.ds(c * 8, 8), :],
-                planes_ref.at[half * FOUR + group],
-            )
-
-    def body(group, carry):
+    half_kernel(other_ref, planes_ref)
+
+    def own_body(group, carry):
         total = forward_maps(
-            planes_ref.at[group], pack_ref, state_ref.at[group], own_bump(group)
+            planes_own_ref.at[group], pack_ref, state_ref.at[group], own_bump(group)
         )
         keep_total(totals_ref, group, total)
-        keep_planes(planes_ref, state_ref, group)
+        keep_planes(planes_own_ref, group, state_ref, group)
         copy_out(state_ref, state_hbm, sems, group).start()
         return carry
 
-    lax.fori_loop(0, 8, body, 0)
+    def other_body(group, carry):
+        place = FOUR + group
+        total = forward_maps(planes_ref.at[group], pack_ref, state_ref.at[place], None)
+        keep_total(totals_ref, place, total)
+        keep_planes(planes_ref, group, state_ref, place)
+        copy_out(state_ref, state_hbm, sems, place).start()
+        return carry
+
+    lax.fori_loop(0, FOUR, own_body, 0)
+    lax.fori_loop(0, FOUR, other_body, 0)
     entries = sum_entries(totals_ref)
     lane = lane_index((8, LANES))
     turned = jnp.where(lane < 16, pltpu.roll(entries, LANES - 16, 1), pltpu.roll(entries, 16, 1))
@@ -352,10 +365,14 @@
     both = entries + pltpu.roll(entries_t_ref[...], SIDE, 1)
     both = both + pltpu.roll(pltpu.roll(both, 64, 1), FOUR, 0)
     both = pltpu.roll(both, SIDE * (lax.axis_index("tgt") % FOUR), 1)
-    for d in range(payload_ref.shape[0]):
-        payload_ref[d] = both[:FOUR]
+    both = jnp.concatenate([both[:FOUR], both[:FOUR]], axis=0)
+    for d in range(payload_ref.shape[0] // 8):
+        payload_ref[pl.ds(8 * d, 8), :] = both
+    payload_out = pltpu.make_async_copy(payload_ref, payload_hbm, sems.at[8])
+    payload_out.start()
     for group in range(8):
         copy_out(state_ref, state_hbm, sems, group).wait()
+    payload_out.wait()
 
 
 def units_kernel(state_t_hbm, state_s_hbm, units_hbm, state_ref, units_ref, in_sems, out_sems):
@@ -442,7 +459,7 @@
 def solve_kernel(
     own_ref,
     other_ref,
-    support_labels_ref,
+    support_labels_hbm,
     columns_ref,
     pack_hbm,
     units_hbm,
@@ -450,6 +467,7 @@
     state_s_hbm,
     grad_hbm,
     objective_ref,
+    support_labels_ref,
     grad_ref,
     inverses_ref,
     units_ref,
@@ -473,6 +491,7 @@
                 (units_hbm, units_ref),
                 (state_t_hbm.at[:, pl.ds(6 * SIDE, SIDE + 12)], second_ref.at[pl.ds(0, 8)]),
                 (state_s_hbm.at[:, pl.ds(6 * SIDE, SIDE + 12)], second_ref.at[pl.ds(8, 8)]),
+                (support_labels_hbm, support_labels_ref),
             ]
         )
     ]
@@ -556,7 +575,14 @@
         hot = (class_id == labels).astype(jnp.float32) - 0.1
         return jnp.where(class_id < CLASSES, hot, 0.0)
 
-    support_hot = one_hot(support_labels_ref[...])
+    copies[-1].wait()
+    natural = jnp.where(
+        class_id < CLASSES, (class_id == support_labels_ref[...]).astype(jnp.float32), 0.0
+    )
+    member = col_id % SIDE
+    source = col_id - member + 2 * (member % 16) + member // 16
+    support_hot = dot(natural.astype(jnp.bfloat16), (row_id == source).astype(jnp.bfloat16))
+    support_hot = jnp.where(class_id < CLASSES, support_hot - 0.1, 0.0)
     lane1 = lane_index((1, LANES))
     halves = []
     for h in range(2):
@@ -632,7 +658,7 @@
         weights_ref[g] = wide[:8, g * LANES : (g + 1) * LANES]
         weights_ref[8 + lax.rem(g + FOUR * core, 8)] = wide[8:, g * LANES : (g + 1) * LANES]
 
-    for copy in copies:
+    for copy in copies[:-1]:
         copy.wait()
 
     block = lane8 // SIDE
@@ -661,7 +687,7 @@
             grads_ref[n, s] = merge_blocks(lines[n], block)
         return carry
 
-    lax.fori_loop(0, 8, gather_line, 0, unroll=4)
+    lax.fori_loop(0, 8, gather_line, 0, unroll=8)
 
     masks = edge_masks((8, LANES))
 
@@ -681,7 +707,7 @@
             grad_ref[pl.ds(c * 8 + s, 8, stride=24), :] = (
                 grads_ref[c, s] + (2.0 * FIRST) * first[s] * image
             )
-    copy = pltpu.make_async_copy(grad_ref, grad_hbm, sems.at[5])
+    copy = pltpu.make_async_copy(grad_ref, grad_hbm, sems.at[6])
     copy.start()
     copy.wait()
 
@@ -713,6 +739,11 @@
 WORK = 256 * 1024 * 140
 
 
+def spread(x, axes, pieces, **groups):
+    moved = lax.all_to_all(x.reshape(pieces, -1), axes, 0, 0, tiled=True, **groups)
+    return moved.reshape(x.shape)
+
+
 def on_device(support, support_labels, targets, target_labels):
     scratch = pltpu.VMEM
     zx = [[2 * m + core for m in range(16)] for core in range(2)]
@@ -720,17 +751,14 @@
     cores = [(device, device ^ 1) for device in range(32)]
 
     image = support.reshape(24, LANES)
-    column_message = call(
-        message_kernel, [VMEM] * 2, VMEM, f32(8, 32, LANES), [], 60 * KIB
+    column_message, row_message = call(
+        message_kernel, [VMEM] * 2, [VMEM] * 2, [f32(8, 32, LANES), f32(16, 24, LANES)], [], 60 * KIB
     )(image, target_labels.reshape(1, 32))
     columns = lax.all_to_all(column_message, "tgt", 0, 0, tiled=True).reshape(256, LANES)
-    planes_t, row_message = call(
-        row_kernel, [VMEM] * 2, [VMEM] * 2, [f32(*PLANES), f32(16, 24, LANES)], [], 48 * KIB, WORK // 2
-    )(targets.transpose(1, 0, 2), image)
-    labels = support_labels.reshape(8, 16, 2).transpose(0, 2, 1).reshape(1, 256)
-    columns, planes_t, row_message, labels = lax.optimization_barrier(
-        (columns, planes_t, row_message, labels)
+    planes_t = call(row_kernel, [VMEM], VMEM, f32(*PLANES), [], 48 * KIB, WORK // 2)(
+        targets.transpose(1, 0, 2)
     )
+    columns, planes_t, row_message = lax.optimization_barrier((columns, planes_t, row_message))
     rows = lax.all_to_all(row_message, "sup", 0, 0, tiled=True, axis_index_groups=zx)
     entries_t, pack, state_t = call(
         target_kernel,
@@ -747,21 +775,25 @@
     )(planes_t, columns)
     rows, entries_t = lax.optimization_barrier((rows, entries_t))
     rows_other = lax.ppermute(rows, "sup", cores)
+    planes_own = call(
+        half_kernel, [VMEM], VMEM, f32(FOUR, *PLANES[1:]), [], 48 * KIB, WORK // 2
+    )(rows)
     payload, state_s = call(
         entries_kernel,
         [VMEM] * 4,
-        [VMEM, HBM],
-        [f32(128, FOUR, LANES), f32(*STATE)],
+        [HBM] * 2,
+        [f32(512, LANES), f32(*STATE)],
         [
-            scratch(PLANES, jnp.float32),
+            scratch((FOUR, *PLANES[1:]), jnp.float32),
             scratch(STATE, jnp.float32),
             scratch((8, 1024), jnp.float32),
-            pltpu.SemaphoreType.DMA((8,)),
+            scratch((512, LANES), jnp.float32),
+            pltpu.SemaphoreType.DMA((9,)),
         ],
         52500,
         WORK // 2,
-    )(rows, rows_other, pack, entries_t)
-    received = lax.all_to_all(payload, BOTH, 0, 0, tiled=True, axis_index_groups=chips)
+    )(planes_own, rows_other, pack, entries_t)
+    received = spread(payload, BOTH, 128, axis_index_groups=chips)
     units = call(
         units_kernel,
         [HBM] * 2,
@@ -780,10 +812,11 @@
     received_other = lax.ppermute(received, "sup", cores)
     partial, objective = call(
         solve_kernel,
-        [VMEM] * 4 + [HBM] * 4,
+        [VMEM] * 2 + [HBM, VMEM] + [HBM] * 4,
         [HBM, VMEM],
         [f32(192, LANES), f32(8, LANES)],
         [
+            scratch((1, 256), jnp.int32),
             scratch((192, LANES), jnp.float32),
             scratch((2, SIDE, 8, LANES), jnp.float32),
             scratch((16, 2 * SIDE, 8, LANES), jnp.float32),
@@ -795,14 +828,14 @@
             scratch((2, 256, 256), jnp.bfloat16),
             scratch((16, 8, LANES), jnp.float32),
             scratch((5, 8, 8, LANES), jnp.float32),
-            pltpu.SemaphoreType.DMA((6,)),
+            pltpu.SemaphoreType.DMA((7,)),
         ],
         54200,
         WORK,
     )(
-        received.reshape(512, LANES),
-        received_other.reshape(512, LANES),
-        labels,
+        received,
+        received_other,
+        support_labels.reshape(1, 256),
         columns,
         pack,
         units,

time: 88.5 us -> 87.1 us (0.984)
  waiting for transfers between devices: 17.7 us -> 19.9 us
  local copies, waits for them, and re-layouts: 3.25 us -> 1.52 us
  Pallas kernels: 34 us -> 32.4 us
    all_to_all x1, waiting for transfers between devices: 3.14 us -> 5.47 us  [on_device(): lax.all_to_all(column_message, 'tgt', 0, 0, tiled=True).reshape(256, LANES)]
    pallas_call x4 -> x5, Pallas kernels: 17.9 us -> 16.4 us  [the longest x1 8.34 us: on_device(): call(solve_kernel, [VMEM] * 2 + [HBM, VMEM] + [HBM] * 4, [HBM, VMEM], [f3...]
    reshape x2 -> x0, local copies, waits for them, and re-layouts: 0.9 us -> none  [on_device(): labels = support_labels.reshape(8, 16, 2).transpose(0, 2, 1).reshape(1, 256)]
  transfers between devices with their start and end apart: 6 -> 6, of which waited for: 6 -> 6; matrix products, arithmetic and copies ran while one was open for 2% -> 1% of each run, Pallas kernels for 20% -> 20%
where the time goes in v4:
time: 87.1 us; the launch traced here: 86.4 us
  Pallas kernels  32.4 us (37%)
  starting transfers between devices  31.3 us (36%)
  waiting for transfers between devices  19.9 us (23%)
  local copies, waits for them, and re-layouts  1.52 us (2%)
    pallas_call x1, Pallas kernels, on_device(): call(units_kernel, [HBM] * 2, HBM, f32(*UNITS), [scratch((16, 6 * SIDE, 8...  10.4 us
    pallas_call x1, Pallas kernels, on_device(): call(solve_kernel, [VMEM] * 2 + [HBM, VMEM] + [HBM] * 4, [HBM, VMEM], [f3...  8.34 us
    all_to_all x1, starting transfers between devices, on_device(): lax.all_to_all(row_message, 'sup', 0, 0, tiled=True, axis_index_groups=zx)  8.32 us
    all_to_all x1, starting transfers between devices, on_device(): lax.all_to_all(column_message, 'tgt', 0, 0, tiled=True).reshape(256, LANES)  7.48 us
    all_to_all x1, waiting for transfers between devices, on_device(): lax.all_to_all(partial.reshape(8, 24, LANES), 'tgt', 0, 0, tiled=True)  6.31 us
    all_to_all x1, starting transfers between devices, spread(): lax.all_to_all(x.reshape(pieces, -1), axes, 0, 0, tiled=True, **groups)  6.17 us
    pallas_call x1, Pallas kernels, on_device(): call(entries_kernel, [VMEM] * 4, [HBM] * 2, [f32(512, LANES), f32(*STATE)...  5.71 us
    pallas_call x1, Pallas kernels, on_device(): call(target_kernel, [VMEM] * 2, [VMEM] * 2 + [HBM], [f32(8, LANES), f32(*...  5.65 us
  transfers between devices with their start and end apart: 6, of which 6 were waited for; matrix products, arithmetic and copies ran while one was open for 1% of the time, Pallas kernels for 20%

profile of v4, /device:TPU:1, one launch (start us, length us, event | category | flops | bytes accessed | tf_op | source)
XLA Modules:
  0.0 86.4 jit_solution(4950914202614375545)
XLA Ops:
  0.6 1.5 %shard_map.59 = (f32[8,32,128]{2,1,0:T(8,128)}, f32[16,24,128]{2,1,0:T(8,128)}) custom-call(f32[24,128]{1,0:T(8,128)} %bitcast.17, s32[1,32]{1,0:T(1,128)} %bitcast.18), custom_call_target="tpu_custom_call" | custom-call | bytes 4194304 | tf_op jit(solution)/shard_map/pallas_call | solution.py:754
  2.1 7.5 %all-to-all-start = ((f32[8,32,128]{2,1,0:T(8,128)}), f32[8,32,128]{2,1,0:T(8,128)S(1)}, u32[]{:S(2)}, u32[]{:S(2)}) async-start(f32[8,32,128]{2,1,0:T(8,128)} %get-tuple-element.18), calls=%async_computation | async-start | bytes 262144 | tf_op jit(solution)/shard_map/all_to_all | solution.py:757
  9.6 1.0 %copy-done.1 = f32[32,3,1024]{2,0,1:T(8,128)S(1)} copy-done((f32[32,3,1024]{2,0,1:T(8,128)S(1)}, f32[32,3,1024]{2,0,1:T(8,128)}, u32[]{:S(2)}) %copy-start.1) | copy-done | bytes 393240
  10.6 0.6 shard_map.60.planes_ref
  11.2 5.5 %all-to-all-done = f32[8,32,128]{2,1,0:T(8,128)S(1)} async-done(((f32[8,32,128]{2,1,0:T(8,128)}), f32[8,32,128]{2,1,0:T(8,128)S(1)}, u32[]{:S(2)}, u32[]{:S(2)}) %all-to-all-start) | async-done | bytes 131104 | tf_op jit(solution)/shard_map/all_to_all | solution.py:757
  16.7 8.3 %all-to-all-start.1 = ((f32[16,24,128]{2,1,0:T(8,128)}), f32[16,24,128]{2,1,0:T(8,128)S(1)}, u32[]{:S(2)}, u32[]{:S(2)}) async-start(f32[16,24,128]{2,1,0:T(8,128)} %get-tuple-element.20), calls=%async_computation.1 | async-start | bytes 393216 | tf_op jit(solution)/shard_map/all_to_all | solution.py:762
  25.0 5.7 %shard_map.61 = (f32[8,128]{1,0:T(8,128)S(1)}, f32[7,32,8,128]{3,2,1,0:T(8,128)S(1)}, f32[8,236,8,128]{3,2,1,0:T(8,128)}) custom-call(f32[8,7,4,8,128]{4,3,2,1,0:T(8,128)S(1)} %shard_map.60.planes_ref, f32[256,128]{1,0:T(8,128)S(1)} %bitcast.10), custom_call_target="tpu_custom_call" | custom-call | flops 36700160 | bytes 4194304 | tf_op jit(solution)/shard_map/pallas_call | solution.py:763
  30.7 0.0 copy-start
  30.7 3.4 %all-to-all-done.1.images_ref = f32[16,24,128]{2,1,0:T(8,128)S(1)} async-done(((f32[16,24,128]{2,1,0:T(8,128)}), f32[16,24,128]{2,1,0:T(8,128)S(1)}, u32[]{:S(2)}, u32[]{:S(2)}) %all-to-all-start.1) | async-done | bytes 196640 | tf_op jit(solution)/shard_map/all_to_all | solution.py:762
  34.0 3.5 %collective-permute-start = (f32[16,24,128]{2,1,0:T(8,128)S(1)}, f32[16,24,128]{2,1,0:T(8,128)S(1)}, u32[]{:S(2)}, u32[]{:S(2)}) collective-permute-start(f32[16,24,128]{2,1,0:T(8,128)S(1)} %all-to-all-done.1.images_ref), channel_id=1, source_target_pairs={{0,1},{1,0},{2,3},{3,2},{4,5},{5,4},{6,7},{7,6},{8,9},{9,8},{10,11... | collective-permute-start | bytes 589832 | tf_op jit(solution)/shard_map/ppermute | solution.py:777
  37.6 0.3 shard_map.62.planes_own_ref
  37.9 0.8 collective-permute-done.other_ref
  38.6 5.7 %shard_map.63 = (f32[512,128]{1,0:T(8,128)}, f32[8,236,8,128]{3,2,1,0:T(8,128)}) custom-call(f32[4,7,4,8,128]{4,3,2,1,0:T(8,128)S(1)} %shard_map.62.planes_own_ref, f32[16,24,128]{2,1,0:T(8,128)S(1)} %collective-permute-done.other_ref, f32[7,32,8,128]{3,2,1,0:T(8,128)S(1)} %get-tuple-element.25.pack_ref.pack_hbm, f32[8,128]{1,0:T(8,128)S(1)} %get-tuple-element.26.entries_t_ref), custom_call_target="tpu_custom_call" | custom-call | flops 18350080 | bytes 4194304 | tf_op jit(solution)/shard_map/pallas_call | solution.py:781
  44.4 6.2 %all-to-all-start.2 = ((f32[128,1,512]{2,1,0:T(1,128)}), f32[128,1,512]{2,1,0:T(1,128)S(1)}, u32[]{:S(2)}, u32[]{:S(2)}) async-start(f32[128,1,512]{2,1,0:T(1,128)} %bitcast.4), calls=%async_computation.2 | async-start | bytes 524288 | tf_op jit(solution)/shard_map/all_to_all | solution.py:743
  50.5 0.0 copy-start.2
  50.5 10.4 %shard_map.64.units_hbm = f32[16,64,8,128]{3,2,1,0:T(8,128)} custom-call(f32[8,236,8,128]{3,2,1,0:T(8,128)} %get-tuple-element.28.state_t_hbm, f32[8,236,8,128]{3,2,1,0:T(8,128)} %get-tuple-element.29.state_s_hbm), custom_call_target="tpu_custom_call" | custom-call | flops 36700160 | bytes 4194304 | tf_op jit(solution)/shard_map/pallas_call | solution.py:797
  60.9 2.8 %all-to-all-done.2 = f32[128,1,512]{2,1,0:T(1,128)S(1)} async-done(((f32[128,1,512]{2,1,0:T(1,128)}), f32[128,1,512]{2,1,0:T(1,128)S(1)}, u32[]{:S(2)}, u32[]{:S(2)}) %all-to-all-start.2) | async-done | bytes 262176 | tf_op jit(solution)/shard_map/all_to_all | solution.py:743
  63.7 2.4 %collective-permute-start.1 = (f32[512,128]{1,0:T(8,128)S(1)}, f32[512,128]{1,0:T(8,128)S(1)}, u32[]{:S(2)}, u32[]{:S(2)}) collective-permute-start(f32[512,128]{1,0:T(8,128)S(1)} %bitcast.12), channel_id=1, source_target_pairs={{0,1},{1,0},{2,3},{3,2},{4,5},{5,4},{6,7},{7,6},{8,9},{9,8},{10,11... | collective-permute-start | bytes 786440 | tf_op jit(solution)/shard_map/ppermute | solution.py:812
  66.1 1.2 %collective-permute-done.1.other_ref = f32[512,128]{1,0:T(8,128)S(1)} collective-permute-done((f32[512,128]{1,0:T(8,128)S(1)}, f32[512,128]{1,0:T(8,128)S(1)}, u32[]{:S(2)}, u32[]{:S(2)}) %collective-permute-start.1) | collective-permute-done | bytes 262176 | tf_op jit(solution)/shard_map/ppermute | solution.py:812
  67.3 8.3 %shard_map.65 = (f32[192,128]{1,0:T(8,128)}, f32[8,128]{1,0:T(8,128)S(1)}) custom-call(f32[512,128]{1,0:T(8,128)S(1)} %bitcast.13, f32[512,128]{1,0:T(8,128)S(1)} %collective-permute-done.1.other_ref, s32[1,256]{1,0:T(1,128)S(1)} %bitcast.15, f32[256,128]{1,0:T(8,128)S(1)} %bitcast.11, f32[7,32,8,128]{3,2,1,0:T(8,128)} %copy-done, ...), custom_call_target="tpu_custom_call" | custom-call | flops 36700160 | bytes 4194304 | tf_op jit(solution)/shard_map/pallas_call | solution.py:813
  75.6 3.4 %all-to-all-start.3 = ((f32[8,24,128]{2,1,0:T(8,128)}), f32[8,24,128]{2,1,0:T(8,128)S(1)}, u32[]{:S(2)}, u32[]{:S(2)}) async-start(f32[8,24,128]{2,1,0:T(8,128)} %bitcast.7), calls=%async_computation.3 | async-start | bytes 196608 | tf_op jit(solution)/shard_map/all_to_all | solution.py:845
  79.0 0.5 slice.3
  79.5 6.3 %all-to-all-done.3 = f32[8,24,128]{2,1,0:T(8,128)S(1)} async-done(((f32[8,24,128]{2,1,0:T(8,128)}), f32[8,24,128]{2,1,0:T(8,128)S(1)}, u32[]{:S(2)}, u32[]{:S(2)}) %all-to-all-start.3) | async-done | bytes 98336 | tf_op jit(solution)/shard_map/all_to_all | solution.py:845
  85.8 0.6 reduce_sum.9
  (3 shorter events, 0.0 us)
Async XLA Ops:
  2.1 14.5 %all-to-all-start = ((f32[8,32,128]{2,1,0:T(8,128)}), f32[8,32,128]{2,1,0:T(8,128)S(1)}, u32[]{:S(2)}, u32[]{:S(2)}) async-start(f32[8,32,128]{2,1,0:T(8,128)} %get-tuple-element.18), calls=%async_computation | async-start | bytes 262144 | tf_op jit(solution)/shard_map/all_to_all | solution.py:757
  9.6 1.0 %copy-start.1 = (f32[32,3,1024]{2,0,1:T(8,128)S(1)}, f32[32,3,1024]{2,0,1:T(8,128)}, u32[]{:S(2)}) copy-start(f32[32,3,1024]{2,0,1:T(8,128)} %param.6) | copy-start | bytes 1179652
  16.7 17.4 %all-to-all-start.1 = ((f32[16,24,128]{2,1,0:T(8,128)}), f32[16,24,128]{2,1,0:T(8,128)S(1)}, u32[]{:S(2)}, u32[]{:S(2)}) async-start(f32[16,24,128]{2,1,0:T(8,128)} %get-tuple-element.20), calls=%async_computation.1 | async-start | bytes 393216 | tf_op jit(solution)/shard_map/all_to_all | solution.py:762
  30.7 30.2 %copy-start = (f32[7,32,8,128]{3,2,1,0:T(8,128)}, f32[7,32,8,128]{3,2,1,0:T(8,128)S(1)}, u32[]{:S(2)}) copy-start(f32[7,32,8,128]{3,2,1,0:T(8,128)S(1)} %get-tuple-element.25.pack_ref.pack_hbm) | copy-start | bytes 2752516
  34.0 4.6 %collective-permute-start = (f32[16,24,128]{2,1,0:T(8,128)S(1)}, f32[16,24,128]{2,1,0:T(8,128)S(1)}, u32[]{:S(2)}, u32[]{:S(2)}) collective-permute-start(f32[16,24,128]{2,1,0:T(8,128)S(1)} %all-to-all-done.1.images_ref), channel_id=1, source_target_pairs={{0,1},{1,0},{2,3},{3,2},{4,5},{5,4},{6,7},{7,6},{8,9},{9,8},{10,11... | collective-permute-start | bytes 589832 | tf_op jit(solution)/shard_map/ppermute | solution.py:777
  44.4 19.4 %all-to-all-start.2 = ((f32[128,1,512]{2,1,0:T(1,128)}), f32[128,1,512]{2,1,0:T(1,128)S(1)}, u32[]{:S(2)}, u32[]{:S(2)}) async-start(f32[128,1,512]{2,1,0:T(1,128)} %bitcast.4), calls=%async_computation.2 | async-start | bytes 524288 | tf_op jit(solution)/shard_map/all_to_all | solution.py:743
  50.5 16.7 %copy-start.2 = (s32[256]{0:T(256)S(1)}, s32[256]{0:T(256)}, u32[]{:S(2)}) copy-start(s32[256]{0:T(256)} %param.5) | copy-start | bytes 3076
  63.7 3.6 %collective-permute-start.1 = (f32[512,128]{1,0:T(8,128)S(1)}, f32[512,128]{1,0:T(8,128)S(1)}, u32[]{:S(2)}, u32[]{:S(2)}) collective-permute-start(f32[512,128]{1,0:T(8,128)S(1)} %bitcast.12), channel_id=1, source_target_pairs={{0,1},{1,0},{2,3},{3,2},{4,5},{5,4},{6,7},{7,6},{8,9},{9,8},{10,11... | collective-permute-start | bytes 786440 | tf_op jit(solution)/shard_map/ppermute | solution.py:812
  75.6 10.2 %all-to-all-start.3 = ((f32[8,24,128]{2,1,0:T(8,128)}), f32[8,24,128]{2,1,0:T(8,128)S(1)}, u32[]{:S(2)}, u32[]{:S(2)}) async-start(f32[8,24,128]{2,1,0:T(8,128)} %bitcast.7), calls=%async_computation.3 | async-start | bytes 196608 | tf_op jit(solution)/shard_map/all_to_all | solution.py:845

commit v5 on v4

--- a/solution.py
+++ b/solution.py
@@ -323,8 +323,16 @@
         )
 
 
+def own_kernel(images_ref, pack_ref, planes_ref, state_ref, total_ref):
+    half_kernel(images_ref, planes_ref)
+    total_ref[...] = forward_maps(planes_ref.at[0], pack_ref, state_ref.at[0], own_bump(0))
+    keep_planes(planes_ref, 0, state_ref, 0)
+
+
 def entries_kernel(
     planes_own_ref,
+    first_state_ref,
+    first_total_ref,
     other_ref,
     pack_ref,
     entries_t_ref,
@@ -336,6 +344,9 @@
     payload_ref,
     sems,
 ):
+    first_out = copy_out(first_state_ref, state_hbm, sems, 0)
+    first_out.start()
+    totals_ref[:, :LANES] = first_total_ref[...]
     half_kernel(other_ref, planes_ref)
 
     def own_body(group, carry):
@@ -355,7 +366,7 @@
         copy_out(state_ref, state_hbm, sems, place).start()
         return carry
 
-    lax.fori_loop(0, FOUR, own_body, 0)
+    lax.fori_loop(1, FOUR, own_body, 0)
     lax.fori_loop(0, FOUR, other_body, 0)
     entries = sum_entries(totals_ref)
     lane = lane_index((8, LANES))
@@ -775,12 +786,18 @@
     )(planes_t, columns)
     rows, entries_t = lax.optimization_barrier((rows, entries_t))
     rows_other = lax.ppermute(rows, "sup", cores)
-    planes_own = call(
-        half_kernel, [VMEM], VMEM, f32(FOUR, *PLANES[1:]), [], 48 * KIB, WORK // 2
-    )(rows)
+    planes_own, first_state, first_total = call(
+        own_kernel,
+        [VMEM] * 2,
+        [VMEM] * 3,
+        [f32(FOUR, *PLANES[1:]), f32(1, *STATE[1:]), f32(8, LANES)],
+        [],
+        48 * KIB,
+        WORK // 2,
+    )(rows, pack)
     payload, state_s = call(
         entries_kernel,
-        [VMEM] * 4,
+        [VMEM] * 6,
         [HBM] * 2,
         [f32(512, LANES), f32(*STATE)],
         [
@@ -790,9 +807,9 @@
             scratch((512, LANES), jnp.float32),
             pltpu.SemaphoreType.DMA((9,)),
         ],
-        52500,
+        51400,
         WORK // 2,
-    )(planes_own, rows_other, pack, entries_t)
+    )(planes_own, first_state, first_total, rows_other, pack, entries_t)
     received = spread(payload, BOTH, 128, axis_index_groups=chips)
     units = call(
         units_kernel,

time: 87.1 us -> 86.7 us (level)
  no operation moved by 1% of the time
where the time goes in v5:
time: 86.7 us; the launch traced here: 86.1 us
  Pallas kernels  32.5 us (37%)
  starting transfers between devices  31.5 us (36%)
  waiting for transfers between devices  19.3 us (22%)
  local copies, waits for them, and re-layouts  1.52 us (2%)
    pallas_call x1, Pallas kernels, on_device(): call(units_kernel, [HBM] * 2, HBM, f32(*UNITS), [scratch((16, 6 * SIDE, 8...  10.4 us
    pallas_call x1, Pallas kernels, on_device(): call(solve_kernel, [VMEM] * 2 + [HBM, VMEM] + [HBM] * 4, [HBM, VMEM], [f3...  8.32 us
    all_to_all x1, starting transfers between devices, on_device(): lax.all_to_all(row_message, 'sup', 0, 0, tiled=True, axis_index_groups=zx)  8.32 us
    all_to_all x1, starting transfers between devices, on_device(): lax.all_to_all(column_message, 'tgt', 0, 0, tiled=True).reshape(256, LANES)  7.48 us
    all_to_all x1, starting transfers between devices, spread(): lax.all_to_all(x.reshape(pieces, -1), axes, 0, 0, tiled=True, **groups)  6.33 us
    all_to_all x1, waiting for transfers between devices, on_device(): lax.all_to_all(partial.reshape(8, 24, LANES), 'tgt', 0, 0, tiled=True)  6.31 us
    pallas_call x1, Pallas kernels, on_device(): call(target_kernel, [VMEM] * 2, [VMEM] * 2 + [HBM], [f32(8, LANES), f32(*...  5.83 us
    all_to_all x1, waiting for transfers between devices, on_device(): lax.all_to_all(column_message, 'tgt', 0, 0, tiled=True).reshape(256, LANES)  5.47 us
  transfers between devices with their start and end apart: 6, of which 6 were waited for; matrix products, arithmetic and copies ran while one was open for 1% of the time, Pallas kernels for 20%

profile of v5, /device:TPU:1, one launch (start us, length us, event | category | flops | bytes accessed | tf_op | source)
XLA Modules:
  0.0 86.1 jit_solution(11497789990616777738)
XLA Ops:
  0.6 1.5 %shard_map.59 = (f32[8,32,128]{2,1,0:T(8,128)}, f32[16,24,128]{2,1,0:T(8,128)}) custom-call(f32[24,128]{1,0:T(8,128)} %bitcast.17, s32[1,32]{1,0:T(1,128)} %bitcast.18), custom_call_target="tpu_custom_call" | custom-call | bytes 4194304 | tf_op jit(solution)/shard_map/pallas_call | solution.py:765
  2.1 7.5 %all-to-all-start = ((f32[8,32,128]{2,1,0:T(8,128)}), f32[8,32,128]{2,1,0:T(8,128)S(1)}, u32[]{:S(2)}, u32[]{:S(2)}) async-start(f32[8,32,128]{2,1,0:T(8,128)} %get-tuple-element.21), calls=%async_computation | async-start | bytes 262144 | tf_op jit(solution)/shard_map/all_to_all | solution.py:768
  9.6 1.0 %copy-done.1 = f32[32,3,1024]{2,0,1:T(8,128)S(1)} copy-done((f32[32,3,1024]{2,0,1:T(8,128)S(1)}, f32[32,3,1024]{2,0,1:T(8,128)}, u32[]{:S(2)}) %copy-start.1) | copy-done | bytes 393240
  10.6 0.6 shard_map.60.planes_ref
  11.2 5.5 %all-to-all-done = f32[8,32,128]{2,1,0:T(8,128)S(1)} async-done(((f32[8,32,128]{2,1,0:T(8,128)}), f32[8,32,128]{2,1,0:T(8,128)S(1)}, u32[]{:S(2)}, u32[]{:S(2)}) %all-to-all-start) | async-done | bytes 131104 | tf_op jit(solution)/shard_map/all_to_all | solution.py:768
  16.7 8.3 %all-to-all-start.1 = ((f32[16,24,128]{2,1,0:T(8,128)}), f32[16,24,128]{2,1,0:T(8,128)S(1)}, u32[]{:S(2)}, u32[]{:S(2)}) async-start(f32[16,24,128]{2,1,0:T(8,128)} %get-tuple-element.23), calls=%async_computation.1 | async-start | bytes 393216 | tf_op jit(solution)/shard_map/all_to_all | solution.py:773
  25.0 5.8 %shard_map.61 = (f32[8,128]{1,0:T(8,128)S(1)}, f32[7,32,8,128]{3,2,1,0:T(8,128)S(1)}, f32[8,236,8,128]{3,2,1,0:T(8,128)}) custom-call(f32[8,7,4,8,128]{4,3,2,1,0:T(8,128)S(1)} %shard_map.60.planes_ref, f32[256,128]{1,0:T(8,128)S(1)} %bitcast.10), custom_call_target="tpu_custom_call" | custom-call | flops 36700160 | bytes 4194304 | tf_op jit(solution)/shard_map/pallas_call | solution.py:774
  30.9 3.2 %all-to-all-done.1.images_ref = f32[16,24,128]{2,1,0:T(8,128)S(1)} async-done(((f32[16,24,128]{2,1,0:T(8,128)}), f32[16,24,128]{2,1,0:T(8,128)S(1)}, u32[]{:S(2)}, u32[]{:S(2)}) %all-to-all-start.1) | async-done | bytes 196640 | tf_op jit(solution)/shard_map/all_to_all | solution.py:773
  34.0 3.5 %collective-permute-start = (f32[16,24,128]{2,1,0:T(8,128)S(1)}, f32[16,24,128]{2,1,0:T(8,128)S(1)}, u32[]{:S(2)}, u32[]{:S(2)}) collective-permute-start(f32[16,24,128]{2,1,0:T(8,128)S(1)} %all-to-all-done.1.images_ref), channel_id=1, source_target_pairs={{0,1},{1,0},{2,3},{3,2},{4,5},{5,4},{6,7},{7,6},{8,9},{9,8},{10,11... | collective-permute-start | bytes 589832 | tf_op jit(solution)/shard_map/ppermute | solution.py:788
  37.6 0.7 shard_map.62
  38.3 0.4 collective-permute-done.other_ref
  38.7 5.2 %shard_map.63 = (f32[512,128]{1,0:T(8,128)}, f32[8,236,8,128]{3,2,1,0:T(8,128)}) custom-call(f32[4,7,4,8,128]{4,3,2,1,0:T(8,128)S(1)} %get-tuple-element.29.planes_own_ref, f32[1,236,8,128]{3,2,1,0:T(8,128)S(1)} %get-tuple-element.30.first_state_ref, f32[8,128]{1,0:T(8,128)S(1)} %get-tuple-element.31.first_total_ref, ...), custom_call_target="tpu_custom_call" | custom-call | flops 18350080 | bytes 4194304 | tf_op jit(solution)/shard_map/pallas_call | solution.py:798
  43.9 6.3 %all-to-all-start.2 = ((f32[128,1,512]{2,1,0:T(1,128)}), f32[128,1,512]{2,1,0:T(1,128)S(1)}, u32[]{:S(2)}, u32[]{:S(2)}) async-start(f32[128,1,512]{2,1,0:T(1,128)} %bitcast.4), calls=%async_computation.2 | async-start | bytes 524288 | tf_op jit(solution)/shard_map/all_to_all | solution.py:754
  50.2 0.0 copy-start.2
  50.3 10.4 %shard_map.64.units_hbm = f32[16,64,8,128]{3,2,1,0:T(8,128)} custom-call(f32[8,236,8,128]{3,2,1,0:T(8,128)} %get-tuple-element.34.state_t_hbm, f32[8,236,8,128]{3,2,1,0:T(8,128)} %get-tuple-element.35.state_s_hbm), custom_call_target="tpu_custom_call" | custom-call | flops 36700160 | bytes 4194304 | tf_op jit(solution)/shard_map/pallas_call | solution.py:814
  60.6 0.0 copy-done
  60.6 2.8 %all-to-all-done.2 = f32[128,1,512]{2,1,0:T(1,128)S(1)} async-done(((f32[128,1,512]{2,1,0:T(1,128)}), f32[128,1,512]{2,1,0:T(1,128)S(1)}, u32[]{:S(2)}, u32[]{:S(2)}) %all-to-all-start.2) | async-done | bytes 262176 | tf_op jit(solution)/shard_map/all_to_all | solution.py:754
  63.4 2.4 %collective-permute-start.1 = (f32[512,128]{1,0:T(8,128)S(1)}, f32[512,128]{1,0:T(8,128)S(1)}, u32[]{:S(2)}, u32[]{:S(2)}) collective-permute-start(f32[512,128]{1,0:T(8,128)S(1)} %bitcast.12), channel_id=1, source_target_pairs={{0,1},{1,0},{2,3},{3,2},{4,5},{5,4},{6,7},{7,6},{8,9},{9,8},{10,11... | collective-permute-start | bytes 786440 | tf_op jit(solution)/shard_map/ppermute | solution.py:829
  65.8 1.2 %collective-permute-done.1.other_ref = f32[512,128]{1,0:T(8,128)S(1)} collective-permute-done((f32[512,128]{1,0:T(8,128)S(1)}, f32[512,128]{1,0:T(8,128)S(1)}, u32[]{:S(2)}, u32[]{:S(2)}) %collective-permute-start.1) | collective-permute-done | bytes 262176 | tf_op jit(solution)/shard_map/ppermute | solution.py:829
  67.0 8.3 %shard_map.65 = (f32[192,128]{1,0:T(8,128)}, f32[8,128]{1,0:T(8,128)S(1)}) custom-call(f32[512,128]{1,0:T(8,128)S(1)} %bitcast.13, f32[512,128]{1,0:T(8,128)S(1)} %collective-permute-done.1.other_ref, s32[1,256]{1,0:T(1,128)S(1)} %bitcast.15, f32[256,128]{1,0:T(8,128)S(1)} %bitcast.11, f32[7,32,8,128]{3,2,1,0:T(8,128)} %copy-done, ...), custom_call_target="tpu_custom_call" | custom-call | flops 36700160 | bytes 4194304 | tf_op jit(solution)/shard_map/pallas_call | solution.py:830
  75.3 3.4 %all-to-all-start.3 = ((f32[8,24,128]{2,1,0:T(8,128)}), f32[8,24,128]{2,1,0:T(8,128)S(1)}, u32[]{:S(2)}, u32[]{:S(2)}) async-start(f32[8,24,128]{2,1,0:T(8,128)} %bitcast.7), calls=%async_computation.3 | async-start | bytes 196608 | tf_op jit(solution)/shard_map/all_to_all | solution.py:862
  78.7 0.5 slice.3
  79.2 6.3 %all-to-all-done.3 = f32[8,24,128]{2,1,0:T(8,128)S(1)} async-done(((f32[8,24,128]{2,1,0:T(8,128)}), f32[8,24,128]{2,1,0:T(8,128)S(1)}, u32[]{:S(2)}, u32[]{:S(2)}) %all-to-all-start.3) | async-done | bytes 98336 | tf_op jit(solution)/shard_map/all_to_all | solution.py:862
  85.5 0.6 reduce_sum.9
  (3 shorter events, 0.0 us)
Async XLA Ops:
  2.1 14.5 %all-to-all-start = ((f32[8,32,128]{2,1,0:T(8,128)}), f32[8,32,128]{2,1,0:T(8,128)S(1)}, u32[]{:S(2)}, u32[]{:S(2)}) async-start(f32[8,32,128]{2,1,0:T(8,128)} %get-tuple-element.21), calls=%async_computation | async-start | bytes 262144 | tf_op jit(solution)/shard_map/all_to_all | solution.py:768
  9.6 1.0 %copy-start.1 = (f32[32,3,1024]{2,0,1:T(8,128)S(1)}, f32[32,3,1024]{2,0,1:T(8,128)}, u32[]{:S(2)}) copy-start(f32[32,3,1024]{2,0,1:T(8,128)} %param.6) | copy-start | bytes 1179652
  16.7 17.4 %all-to-all-start.1 = ((f32[16,24,128]{2,1,0:T(8,128)}), f32[16,24,128]{2,1,0:T(8,128)S(1)}, u32[]{:S(2)}, u32[]{:S(2)}) async-start(f32[16,24,128]{2,1,0:T(8,128)} %get-tuple-element.23), calls=%async_computation.1 | async-start | bytes 393216 | tf_op jit(solution)/shard_map/all_to_all | solution.py:773
  30.8 29.8 %copy-start = (f32[7,32,8,128]{3,2,1,0:T(8,128)}, f32[7,32,8,128]{3,2,1,0:T(8,128)S(1)}, u32[]{:S(2)}) copy-start(f32[7,32,8,128]{3,2,1,0:T(8,128)S(1)} %get-tuple-element.28.pack_ref.pack_hbm) | copy-start | bytes 2752516
  34.0 4.6 %collective-permute-start = (f32[16,24,128]{2,1,0:T(8,128)S(1)}, f32[16,24,128]{2,1,0:T(8,128)S(1)}, u32[]{:S(2)}, u32[]{:S(2)}) collective-permute-start(f32[16,24,128]{2,1,0:T(8,128)S(1)} %all-to-all-done.1.images_ref), channel_id=1, source_target_pairs={{0,1},{1,0},{2,3},{3,2},{4,5},{5,4},{6,7},{7,6},{8,9},{9,8},{10,11... | collective-permute-start | bytes 589832 | tf_op jit(solution)/shard_map/ppermute | solution.py:788
  43.9 19.5 %all-to-all-start.2 = ((f32[128,1,512]{2,1,0:T(1,128)}), f32[128,1,512]{2,1,0:T(1,128)S(1)}, u32[]{:S(2)}, u32[]{:S(2)}) async-start(f32[128,1,512]{2,1,0:T(1,128)} %bitcast.4), calls=%async_computation.2 | async-start | bytes 524288 | tf_op jit(solution)/shard_map/all_to_all | solution.py:754
  50.2 16.7 %copy-start.2 = (s32[256]{0:T(256)S(1)}, s32[256]{0:T(256)}, u32[]{:S(2)}) copy-start(s32[256]{0:T(256)} %param.5) | copy-start | bytes 3076
  63.4 3.6 %collective-permute-start.1 = (f32[512,128]{1,0:T(8,128)S(1)}, f32[512,128]{1,0:T(8,128)S(1)}, u32[]{:S(2)}, u32[]{:S(2)}) collective-permute-start(f32[512,128]{1,0:T(8,128)S(1)} %bitcast.12), channel_id=1, source_target_pairs={{0,1},{1,0},{2,3},{3,2},{4,5},{5,4},{6,7},{7,6},{8,9},{9,8},{10,11... | collective-permute-start | bytes 786440 | tf_op jit(solution)/shard_map/ppermute | solution.py:829
  75.3 10.2 %all-to-all-start.3 = ((f32[8,24,128]{2,1,0:T(8,128)}), f32[8,24,128]{2,1,0:T(8,128)S(1)}, u32[]{:S(2)}, u32[]{:S(2)}) async-start(f32[8,24,128]{2,1,0:T(8,128)} %bitcast.7), calls=%async_computation.3 | async-start | bytes 196608 | tf_op jit(solution)/shard_map/all_to_all | solution.py:862
